TPU v7x, 32 devices: a whole 2x2x4 slice. The times are simulated.
32 devices in a mesh: vox: 8 (over z, y), ch: 4 (over x, core).
Axes of the slice: x: 2, y: 2, z: 4, core: 2. Of those that a mesh axis runs over, the one named last changes fastest.
Arguments:
- features: bfloat16 [8192, 128], P('vox'), may hold values from -6 to 6
- kernel: bfloat16 [27, 256, 128], P(None, 'ch'), may hold values from -0.1875 to 0.1875
- coarse_grad: bfloat16 [256, 4096], P('ch', 'vox'), may hold values from -6 to 6
- pair_fine: int32 [32768], P('vox'), may hold values from 0 to 1023
- pair_target: int32 [32768], P('vox'), may hold values from 0 to 511
- block_offset: int32 [256], P('vox'), may hold values from 0 to 26
- target_owner: int32 [4096, 1], P('vox'), may hold values from 0 to 7; in each aligned block of 512 rows (0 to 511, 512 to 1023, ...) at most 96 rows name the same one
- slot_coarse_row: int32 [6144], P('vox'), may hold values from 0 to 511
- fine_count: int32 [8], P('vox'), may hold values from 512 to 1024, as said below
Outputs:
- activation: bfloat16 [256, 4096], P('ch', 'vox')
- grad_features: bfloat16 [128, 8192], P('ch', 'vox')
- grad_kernel: bfloat16 [27, 256, 128], P(None, 'ch')
Inputs may be any that keep to these rules, and one draw needn't show every extreme that they name: `target_owner`: among the 512 targets of one block no owner appears more than 96 times, and in some block one owner appears exactly 96 times. `fine_count`: some block has all 1024 fine voxels live.
All inputs are finite; a program needn't handle non-finite values.
Results may differ from a plain program's by a relative error of at most 0.0053.
Values may be sent and summed in bfloat16 or wider, within the bound.
A program may use at most 64 MiB of HBM per device.

v0:
```python
import math

import jax
import jax.numpy as jnp
from jax import lax
from jax.sharding import PartitionSpec as P


def owner_slots(owner_of, owners):
    labels = jnp.arange(owners, dtype=jnp.int32)
    onehot = (owner_of[:, None] == labels[None, :]).astype(jnp.int32)
    before = jnp.cumsum(onehot, axis=0) - onehot
    return jnp.sum(before * onehot, axis=1)


def body(
    features,
    kernel,
    coarse_grad,
    pair_fine,
    pair_target,
    block_offset,
    target_owner,
    slot_coarse_row,
    fine_count,
):
    owners = lax.axis_size("vox")
    fine_total, width_in = features.shape
    width_out, coarse_total = coarse_grad.shape
    offsets_all = kernel.shape[0]
    targets = target_owner.shape[0]
    capacity = slot_coarse_row.shape[0] // owners
    blocks = block_offset.shape[0]
    rows_each_turn = min(16, blocks)
    rounds = blocks // rows_each_turn
    live_mask = jnp.arange(fine_total, dtype=jnp.int32) < fine_count[0]
    masked = jnp.where(live_mask[:, None], features, jnp.zeros((), features.dtype))
    fine_ids = pair_fine.reshape(rounds, rows_each_turn, 128)
    target_ids = pair_target.reshape(rounds, rows_each_turn, 128)
    offset_ids = block_offset.reshape(rounds, rows_each_turn)

    def forward_step(totals, pieces):
        fine_at, target_at, offset_at = pieces
        gathered = masked[fine_at]
        partial_value = jnp.einsum(
            "gpc,goc->gpo", gathered, kernel[offset_at], preferred_element_type=jnp.float32
        )
        return (totals.at[target_at.reshape(-1)].add(partial_value.reshape(-1, width_out)), None)

    target_sum, leftover = lax.scan(
        forward_step,
        jnp.zeros((targets, width_out), jnp.float32),
        (fine_ids, target_ids, offset_ids),
    )
    target_part = target_sum.astype(jnp.bfloat16)
    owner_of = target_owner[:, 0]
    slot_index = owner_of * capacity + owner_slots(owner_of, owners)
    send_rows = (
        jnp.zeros((owners * capacity, width_out), jnp.bfloat16).at[slot_index].set(target_part)
    )
    as_lanes = capacity * width_out % 128 == 0
    lane_shape = (owners * capacity * width_out // 128, 128)
    received = lax.all_to_all(
        send_rows.reshape(lane_shape), "vox", split_axis=0, concat_axis=0, tiled=True
    )
    got_rows = received.reshape(owners * capacity, width_out).astype(jnp.float32)
    coarse = jax.ops.segment_sum(got_rows, slot_coarse_row, coarse_total)
    gate_output = jax.nn.sigmoid(coarse)
    activation = (coarse * gate_output).astype(jnp.bfloat16)
    grad_coarse = (
        coarse_grad.astype(jnp.float32).T * gate_output * (1.0 + coarse * (1.0 - gate_output))
    ).astype(jnp.bfloat16)
    back_rows = grad_coarse[slot_coarse_row]
    returned = lax.all_to_all(
        back_rows.reshape(lane_shape), "vox", split_axis=0, concat_axis=0, tiled=True
    )
    grad_target = returned.reshape(owners * capacity, width_out)[slot_index]
    weight_init = jnp.zeros((offsets_all, width_out, width_in), jnp.float32)

    def reverse_update(state_pair, pieces):
        fine_sum, weight_sum = state_pair
        fine_at, target_at, offset_at = pieces
        gathered = masked[fine_at]
        grad_rows = grad_target[target_at]
        grad_in = jnp.einsum(
            "gpo,goc->gpc", grad_rows, kernel[offset_at], preferred_element_type=jnp.float32
        )
        fine_sum = fine_sum.at[fine_at.reshape(-1)].add(grad_in.reshape(-1, width_in))
        grad_weight = jnp.einsum(
            "gpc,gpo->goc", gathered, grad_rows, preferred_element_type=jnp.float32
        )
        return ((fine_sum, weight_sum.at[offset_at].add(grad_weight)), None)

    (fine_sum, weight_sum), leftover = lax.scan(
        reverse_update,
        (jnp.zeros((fine_total, width_in), jnp.float32), weight_init),
        (fine_ids, target_ids, offset_ids),
    )
    fine_grad = lax.psum_scatter(fine_sum, "ch", scatter_dimension=1, tiled=True)
    grad_features = jnp.where(live_mask[:, None], fine_grad, jnp.zeros((), jnp.float32)).astype(
        jnp.bfloat16
    )
    weight_total = lax.psum(weight_sum, "vox")
    factor = math.sqrt(offsets_all / (blocks * 128 * owners))
    grad_kernel = (weight_total * factor).astype(jnp.bfloat16)
    return (activation.T, grad_features.T, grad_kernel)


def solution(mesh):
    in_specs = (
        P("vox", None),
        P(None, "ch", None),
        P("ch", "vox"),
        P("vox"),
        P("vox"),
        P("vox"),
        P("vox", None),
        P("vox"),
        P("vox"),
    )
    out_specs = (P("ch", "vox"), P("ch", "vox"), P(None, "ch", None))
    return jax.shard_map(body, mesh=mesh, in_specs=in_specs, out_specs=out_specs, check_vma=False)
```

profile of v0, /device:TPU:0, one launch (start us, length us, event | category | flops | bytes accessed | tf_op | source)
XLA Modules:
  0.0 235.7 jit_solution(17541603526647433418)
XLA Ops:
  8.7 1.1 reduce-window.6
  11.6 1.1 broadcast_select_fusion
  13.5 39.6 %while.22 = (s32[]{:T(128)}, f32[512,64]{1,0:T(8,128)S(1)}, s32[2,16,128]{2,1,0:T(8,128)S(1)}, s32[2,16,128]{2,1,0:T(8,128)S(1)}, bf16[1024,128]{1,0:T(8,128)(2,...) while((s32[]{:T(128)}, f32[512,64]{1,0:T(8,128)S(1)}, ...), condition=%wide.region_5.6_spmd, body=%wide.region_3.5_spmd.sunk | while | flops 33700912 | bytes 4526433 | solution.py:50
  13.5 6.2 %gather_fusion = bf16[2048,128]{1,0:T(8,128)(2,1)S(1)} fusion(bf16[1024,128]{1,0:T(8,128)(2,1)S(1)} %get-tuple-element.268, s32[2048]{0:T(1024)S(1)} %fusion.46), kind=kCustom, calls=%fused_computation.clone.1 | custom fusion | bytes 1056768 | tf_op jit(solution)/shard_map/while/body/eval_jaxpr/gather | solution.py:44
  19.7 1.6 gather_fusion.1
  21.6 11.6 %scatter_fusion = f32[512,64]{1,0:T(8,128)S(1)} fusion(f32[512,64]{1,0:T(8,128)S(1)} %get-tuple-element.257, s32[2048]{0:T(1024)S(1)} %bitcast.127, f32[2048,64]{1,0:T(8,128)S(1)} %bitcast.123), kind=kCustom, calls=%fused_computation.7.clone.1 | custom fusion | flops 131072 | bytes 1581056 | tf_op jit(solution)/shard_map/while/body/eval_jaxpr/scatter-add | solution.py:48
  33.3 6.2 %gather_fusion = bf16[2048,128]{1,0:T(8,128)(2,1)S(1)} fusion(bf16[1024,128]{1,0:T(8,128)(2,1)S(1)} %get-tuple-element.268, s32[2048]{0:T(1024)S(1)} %fusion.46), kind=kCustom, calls=%fused_computation.clone.1 | custom fusion | bytes 1056768 | tf_op jit(solution)/shard_map/while/body/eval_jaxpr/gather | solution.py:44
  39.5 1.6 gather_fusion.1
  41.4 11.6 %scatter_fusion = f32[512,64]{1,0:T(8,128)S(1)} fusion(f32[512,64]{1,0:T(8,128)S(1)} %get-tuple-element.257, s32[2048]{0:T(1024)S(1)} %bitcast.127, f32[2048,64]{1,0:T(8,128)S(1)} %bitcast.123), kind=kCustom, calls=%fused_computation.7.clone.1 | custom fusion | flops 131072 | bytes 1581056 | tf_op jit(solution)/shard_map/while/body/eval_jaxpr/scatter-add | solution.py:48
  53.0 1.8 scatter_custom_fusion.3
  55.6 7.4 %all-to-all-start = ((bf16[8,48,128]{2,1,0:T(8,128)(2,1)}), bf16[8,48,128]{2,1,0:T(8,128)(2,1)S(1)}, u32[]{:S(2)}, u32[]{:S(2)}) async-start(bf16[8,48,128]{2,1,0:T(8,128)(2,1)} %all_to_all.12), calls=%async_computation | async-start | bytes 196608 | tf_op jit(solution)/shard_map/all_to_all | solution.py:63
  63.1 7.1 %all-to-all-done = bf16[8,48,128]{2,1,0:T(8,128)(2,1)S(1)} async-done(((bf16[8,48,128]{2,1,0:T(8,128)(2,1)}), bf16[8,48,128]{2,1,0:T(8,128)(2,1)S(1)}, u32[]{:S(2)}, u32[]{:S(2)}) %all-to-all-start) | async-done | bytes 98336 | tf_op jit(solution)/shard_map/all_to_all | solution.py:63
  70.3 6.1 %scatter_custom_fusion.4 = f32[512,64]{1,0:T(8,128)S(1)} fusion(s32[768]{0:T(1024)S(1)} %copy-done.7, f32[768,64]{1,0:T(8,128)S(1)} %reshape.360, f32[]{:T(128)} %constant.32.clone.1), kind=kCustom, calls=%fused_computation.45 | custom fusion | flops 49152 | bytes 131076 | tf_op jit(solution)/shard_map/scatter-add | solution.py:67
  78.0 1.9 gather_fusion.5
  80.7 3.4 %all-to-all-start.1 = ((bf16[8,48,128]{2,1,0:T(8,128)(2,1)}), bf16[8,48,128]{2,1,0:T(8,128)(2,1)S(1)}, u32[]{:S(2)}, u32[]{:S(2)}) async-start(bf16[8,48,128]{2,1,0:T(8,128)(2,1)} %all_to_all.14), calls=%async_computation.1 | async-start | bytes 196608 | tf_op jit(solution)/shard_map/all_to_all | solution.py:74
  84.3 6.8 %all-to-all-done.1 = bf16[8,48,128]{2,1,0:T(8,128)(2,1)S(1)} async-done(((bf16[8,48,128]{2,1,0:T(8,128)(2,1)}), bf16[8,48,128]{2,1,0:T(8,128)(2,1)S(1)}, u32[]{:S(2)}, u32[]{:S(2)}) %all-to-all-start.1) | async-done | bytes 98336 | tf_op jit(solution)/shard_map/all_to_all | solution.py:74
  91.3 1.3 gather_fusion.6
  92.7 57.3 %while.23 = (s32[]{:T(128)}, f32[1024,128]{1,0:T(8,128)S(1)}, f32[27,64,128]{2,1,0:T(8,128)S(1)}, s32[2,16,128]{2,1,0:T(8,128)S(1)}, s32[2,16,128]{2,1,0:T(8,128...) while((s32[]{:T(128)}, f32[1024,128]{1,0:T(8,128)S(1)}, ...), condition=%wide.region_11.12_spmd, body=%wide.region_8.11_spmd.sunk | while | flops 67525680 | bytes 16863716 | solution.py:94
  92.8 6.2 %gather_fusion.2 = bf16[2048,64]{1,0:T(8,128)(2,1)S(1)} fusion(bf16[512,64]{1,0:T(8,128)(2,1)S(1)} %get-tuple-element.297, s32[2048]{0:T(1024)S(1)} %get-tuple-element.246), kind=kCustom, calls=%fused_computation.2.clone.1 | custom fusion | bytes 532480 | tf_op jit(solution)/shard_map/while/body/eval_jaxpr/gather | solution.py:84
  99.0 6.2 %gather_fusion.4 = bf16[2048,128]{1,0:T(8,128)(2,1)S(1)} fusion(bf16[1024,128]{1,0:T(8,128)(2,1)S(1)} %get-tuple-element.300, s32[2048]{0:T(1024)S(1)} %get-tuple-element.247), kind=kCustom, calls=%fused_computation.4.clone.1 | custom fusion | bytes 1056768 | tf_op jit(solution)/shard_map/while/body/eval_jaxpr/gather | solution.py:83
  105.5 1.3 scatter_fusion.2
  107.8 1.6 gather_fusion.3
  109.7 11.7 %scatter_fusion.1 = f32[1024,128]{1,0:T(8,128)S(1)} fusion(f32[1024,128]{1,0:T(8,128)S(1)} %get-tuple-element.283, s32[2048]{0:T(1024)S(1)} %bitcast.128, f32[2048,128]{1,0:T(8,128)S(1)} %bitcast.124), kind=kCustom, calls=%fused_computation.8.clone.1 | custom fusion | flops 262144 | bytes 3153920 | tf_op jit(solution)/shard_map/while/body/eval_jaxpr/scatter-add | solution.py:88
  121.4 6.2 %gather_fusion.2 = bf16[2048,64]{1,0:T(8,128)(2,1)S(1)} fusion(bf16[512,64]{1,0:T(8,128)(2,1)S(1)} %get-tuple-element.297, s32[2048]{0:T(1024)S(1)} %get-tuple-element.246), kind=kCustom, calls=%fused_computation.2.clone.1 | custom fusion | bytes 532480 | tf_op jit(solution)/shard_map/while/body/eval_jaxpr/gather | solution.py:84
  127.6 6.2 %gather_fusion.4 = bf16[2048,128]{1,0:T(8,128)(2,1)S(1)} fusion(bf16[1024,128]{1,0:T(8,128)(2,1)S(1)} %get-tuple-element.300, s32[2048]{0:T(1024)S(1)} %get-tuple-element.247), kind=kCustom, calls=%fused_computation.4.clone.1 | custom fusion | bytes 1056768 | tf_op jit(solution)/shard_map/while/body/eval_jaxpr/gather | solution.py:83
  134.1 1.3 scatter_fusion.2
  136.4 1.6 gather_fusion.3
  138.3 11.7 %scatter_fusion.1 = f32[1024,128]{1,0:T(8,128)S(1)} fusion(f32[1024,128]{1,0:T(8,128)S(1)} %get-tuple-element.283, s32[2048]{0:T(1024)S(1)} %bitcast.128, f32[2048,128]{1,0:T(8,128)S(1)} %bitcast.124), kind=kCustom, calls=%fused_computation.8.clone.1 | custom fusion | flops 262144 | bytes 3153920 | tf_op jit(solution)/shard_map/while/body/eval_jaxpr/scatter-add | solution.py:88
  151.1 1.0 copy.46
  152.1 72.5 %all-reduce.2.cloned.1.call-done = f32[27,64,128]{2,1,0:T(8,128)} async-done(((f32[27,64,128]{2,1,0:T(8,128)}), f32[27,64,128]{2,1,0:T(8,128)}) %all-reduce.2.cloned.1.call-update) | async-done | bytes 884752 | tf_op jit(solution)/shard_map/psum | solution.py:103
  224.6 2.1 multiply_convert_fusion
  226.7 1.5 fusion.17
  (72 shorter events, 11.0 us)
Async XLA Ops:
  8.0 0.7 copy-start.6
  10.8 0.7 copy-start.8
  12.7 0.7 copy-start.3
  12.7 0.7 copy-start.4
  55.6 7.4 %copy-start.7 = (s32[768]{0:T(1024)S(1)}, s32[768]{0:T(1024)}, u32[]{:S(2)}) copy-start(s32[768]{0:T(1024)} %param.20) | copy-start | bytes 9220
  55.6 14.5 %all-to-all-start = ((bf16[8,48,128]{2,1,0:T(8,128)(2,1)}), bf16[8,48,128]{2,1,0:T(8,128)(2,1)S(1)}, u32[]{:S(2)}, u32[]{:S(2)}) async-start(bf16[8,48,128]{2,1,0:T(8,128)(2,1)} %all_to_all.12), calls=%async_computation | async-start | bytes 196608 | tf_op jit(solution)/shard_map/all_to_all | solution.py:63
  76.4 0.8 copy-start.5
  80.7 10.4 %all-to-all-start.1 = ((bf16[8,48,128]{2,1,0:T(8,128)(2,1)}), bf16[8,48,128]{2,1,0:T(8,128)(2,1)S(1)}, u32[]{:S(2)}, u32[]{:S(2)}) async-start(bf16[8,48,128]{2,1,0:T(8,128)(2,1)} %all_to_all.14), calls=%async_computation.1 | async-start | bytes 196608 | tf_op jit(solution)/shard_map/all_to_all | solution.py:74
  84.1 140.5 %all-reduce.2.cloned.1.call-start = ((), (), s32[]{:S(2)}) async-start(), calls=%async_computation.4 | async-start | bytes 1769472 | tf_op jit(solution)/shard_map/psum | solution.py:103
  106.8 0.9 copy-start
  109.7 11.7 %copy-start.1 = (f32[27,64,128]{2,1,0:T(8,128)S(1)}, f32[27,64,128]{2,1,0:T(8,128)}, u32[]{:S(2)}) copy-start(f32[27,64,128]{2,1,0:T(8,128)} %copy-done) | copy-start | bytes 2654212 | tf_op jit(solution)/shard_map/while
  135.5 0.9 copy-start
  138.3 11.7 %copy-start.1 = (f32[27,64,128]{2,1,0:T(8,128)S(1)}, f32[27,64,128]{2,1,0:T(8,128)}, u32[]{:S(2)}) copy-start(f32[27,64,128]{2,1,0:T(8,128)} %copy-done) | copy-start | bytes 2654212 | tf_op jit(solution)/shard_map/while
  150.1 0.9 copy-start.2
  151.0 75.6 %reduce-scatter.2.cloned.1.call-start = ((), (), s32[]{:S(2)}) async-start(), calls=%async_computation.3 | async-start | bytes 655360 | tf_op jit(solution)/shard_map/reduce_scatter | solution.py:99
Sparse Core Ops, SparseCore 0:
  151.1 73.4 all-reduce.1
Sparse Core Ops, SparseCore 1:
  154.0 19.2 reduce-scatter.1
where the time goes:
time: 236 us
  waiting for transfers between devices  86.5 us (37%)
  other arithmetic  64 us (27%)
  local copies, waits for them, and re-layouts  55.7 us (24%)
  between operations  16.3 us (7%)
  starting transfers between devices  11 us (5%)
    psum x1, waiting for transfers between devices, body(): weight_total = lax.psum(weight_sum, 'vox')  72.5 us
    scatter-add x2, other arithmetic, reverse_update(): fine_sum.at[fine_at.reshape(-1)].add(grad_in.reshape(-1, width_in))  23.4 us
    scatter-add x2, other arithmetic, forward_step(): totals.at[target_at.reshape(-1)].add(partial_value.reshape(-1, width_out))  23.2 us
    gather x2, local copies, waits for them, and re-layouts, reverse_update(): grad_rows = grad_target[target_at]  12.4 us
    gather x2, local copies, waits for them, and re-layouts, reverse_update(): gathered = masked[fine_at]  12.4 us
    gather x2, local copies, waits for them, and re-layouts, forward_step(): gathered = masked[fine_at]  12.4 us
    all_to_all x1, starting transfers between devices, body(): lax.all_to_all(send_rows.reshape(lane_shape), 'vox', split_axis=0, concat...  7.41 us
    all_to_all x1, waiting for transfers between devices, body(): lax.all_to_all(send_rows.reshape(lane_shape), 'vox', split_axis=0, concat...  7.09 us
  transfers between devices with their start and end apart: 4, of which 3 were waited for; matrix products, arithmetic and copies ran while one was open for 1% of the time, Pallas kernels for 0%

commit v1 on v0

v1 whole, which is shorter than its diff:
```python
import functools
import math

import jax
import jax.numpy as jnp
from jax import lax
from jax.experimental import pallas as pl
from jax.experimental.pallas import tpu as pltpu
from jax.sharding import PartitionSpec as P

LANES = 128
NT = (((1,), (1,)), ((), ()))
TN = (((0,), (0,)), ((), ()))
F32 = jnp.float32
BF16 = jnp.bfloat16


def dot(a, b, dims=(((1,), (0,)), ((), ()))):
    return lax.dot_general(a, b, dims, preferred_element_type=F32)


def onehot(rows, ids, base=0):
    at = lax.broadcasted_iota(jnp.int32, (rows, ids.shape[1]), 0) + base
    return (at == ids).astype(BF16)


def onehot_rows(rows, ids_ref, first, count):
    return jnp.concatenate(
        [onehot(rows, ids_ref[pl.ds(first + j, 1), :]) for j in range(count)], axis=1
    )


def split(value):
    high = value.astype(BF16)
    low = (value - high.astype(F32)).astype(BF16)
    return jnp.concatenate([high, low], axis=0)


def joined(value):
    half = value.shape[0] // 2
    return value[:half] + value[half:]


def slots_of(owner_row, owners, padded):
    targets = owner_row.shape[1]
    lead = max(owners, 8)
    mine = onehot(lead, owner_row)
    earlier = lax.broadcasted_iota(jnp.int32, (targets, targets), 0)
    later = lax.broadcasted_iota(jnp.int32, (targets, targets), 1)
    before = dot(mine, (earlier < later).astype(BF16))
    rank = jnp.sum(before * mine.astype(F32), axis=0, keepdims=True)
    return owner_row * padded + rank.astype(jnp.int32)


def forward_kernel(count, feat, ker, pf, pt, off, own, live, send, slot_out, g_out, ft):
    fine_total, width_in = feat.shape
    width_out = ker.shape[1]
    targets = own.shape[1]
    owners, _, padded = send.shape
    rows = pf.shape[0]
    lanes = count * LANES
    at = lax.broadcasted_iota(jnp.int32, (fine_total, width_in), 0)
    masked = jnp.where(at < live[0], feat[...].astype(F32), 0.0)
    ft[...] = masked.T.astype(BF16)

    def group(g, total):
        foh = onehot_rows(fine_total, pf, g * count, count)
        gathered = dot(ft[...], foh).astype(BF16)
        g_out[g] = gathered
        part = jnp.concatenate(
            [
                dot(ker[off[g * count + j]], gathered[:, j * LANES : (j + 1) * LANES])
                for j in range(count)
            ],
            axis=1,
        )
        toh = onehot_rows(targets, pt, g * count, count)
        return total + dot(split(part), toh, NT)

    total = lax.fori_loop(
        0, rows // count, group, jnp.zeros((2 * width_out, targets), F32)
    )
    part = joined(total).astype(BF16)
    slot = slots_of(own[...], owners, padded)
    slot_out[...] = slot

    def route(o, carry):
        send[o] = dot(part, onehot(padded, slot, o * padded), NT).astype(BF16)
        return carry

    lax.fori_loop(0, owners, route, 0)


def middle_kernel(recv, slots, cg, act, back):
    owners = recv.shape[0]
    width_out, coarse_total = cg.shape

    def gather(o, total):
        return total + dot(recv[o], onehot(coarse_total, slots[pl.ds(o, 1), :]), NT)

    coarse = lax.fori_loop(0, owners, gather, jnp.zeros((width_out, coarse_total), F32))
    gate = jax.nn.sigmoid(coarse)
    act[...] = (coarse * gate).astype(BF16)
    grad = (cg[...].astype(F32) * gate * (1.0 + coarse * (1.0 - gate))).astype(BF16)

    def give(o, carry):
        back[o] = dot(grad, onehot(coarse_total, slots[pl.ds(o, 1), :])).astype(BF16)
        return carry

    lax.fori_loop(0, owners, give, 0)


def backward_kernel(count, ret, slot, g_in, ker, pf, pt, off, live, fine, weight, acc):
    owners, width_out, padded = ret.shape
    targets = slot.shape[1]
    width_in, fine_total = fine.shape
    rows = pf.shape[0]

    def gather(o, total):
        return total + dot(ret[o], onehot(padded, slot[...], o * padded))

    grad = lax.fori_loop(
        0, owners, gather, jnp.zeros((width_out, targets), F32)
    ).astype(BF16)
    weight[...] = jnp.zeros_like(weight)
    acc[...] = jnp.zeros_like(acc)

    def group(g, carry):
        toh = onehot_rows(targets, pt, g * count, count)
        spread = dot(grad, toh).astype(BF16)
        gathered = g_in[g]
        parts = []
        for j in range(count):
            k = off[g * count + j]
            mine = spread[:, j * LANES : (j + 1) * LANES]
            weight[k] += dot(mine, gathered[:, j * LANES : (j + 1) * LANES], NT)
            parts.append(dot(ker[k], mine, TN))
        foh = onehot_rows(fine_total, pf, g * count, count)
        acc[...] += dot(split(jnp.concatenate(parts, axis=1)), foh, NT)
        return carry

    lax.fori_loop(0, rows // count, group, 0)
    at = lax.broadcasted_iota(jnp.int32, (width_in, fine_total), 1)
    fine[...] = jnp.where(at < live[0], joined(acc[...]), 0.0)


def body(
    features,
    kernel,
    coarse_grad,
    pair_fine,
    pair_target,
    block_offset,
    target_owner,
    slot_coarse_row,
    fine_count,
):
    owners = lax.axis_size("vox")
    fine_total, width_in = features.shape
    width_out, coarse_total = coarse_grad.shape
    offsets_all = kernel.shape[0]
    targets = target_owner.shape[0]
    capacity = slot_coarse_row.shape[0] // owners
    blocks = block_offset.shape[0]
    padded = -(-capacity // LANES) * LANES
    count = 4
    groups = blocks // count
    vm = pl.BlockSpec(memory_space=pltpu.VMEM)
    sm = pl.BlockSpec(memory_space=pltpu.SMEM)
    params = pltpu.CompilerParams(vmem_limit_bytes=48 * 2**20)
    pf = pair_fine.reshape(blocks, LANES)
    pt = pair_target.reshape(blocks, LANES)
    own = target_owner.reshape(1, targets)
    slots = jnp.pad(
        slot_coarse_row.reshape(owners, capacity),
        ((0, 0), (0, padded - capacity)),
        constant_values=-1,
    )
    exchange = jax.ShapeDtypeStruct((owners, width_out, padded), BF16)
    send, slot, gathered = pl.pallas_call(
        functools.partial(forward_kernel, count),
        out_shape=(
            exchange,
            jax.ShapeDtypeStruct((1, targets), jnp.int32),
            jax.ShapeDtypeStruct((groups, width_in, count * LANES), BF16),
        ),
        in_specs=[vm, vm, vm, vm, sm, vm, sm],
        out_specs=(vm, vm, vm),
        scratch_shapes=[pltpu.VMEM((width_in, fine_total), BF16)],
        compiler_params=params,
    )(features, kernel, pf, pt, block_offset, own, fine_count)
    recv = lax.all_to_all(send, "vox", split_axis=0, concat_axis=0, tiled=True)
    activation, back = pl.pallas_call(
        middle_kernel,
        out_shape=(jax.ShapeDtypeStruct((width_out, coarse_total), BF16), exchange),
        in_specs=[vm, vm, vm],
        out_specs=(vm, vm),
        compiler_params=params,
    )(recv, slots, coarse_grad)
    ret = lax.all_to_all(back, "vox", split_axis=0, concat_axis=0, tiled=True)
    fine_sum, weight_sum = pl.pallas_call(
        functools.partial(backward_kernel, count),
        out_shape=(
            jax.ShapeDtypeStruct((width_in, fine_total), F32),
            jax.ShapeDtypeStruct(kernel.shape, F32),
        ),
        in_specs=[vm, vm, vm, vm, vm, vm, sm, sm],
        out_specs=(vm, vm),
        scratch_shapes=[pltpu.VMEM((2 * width_in, fine_total), F32)],
        compiler_params=params,
    )(ret, slot, gathered, kernel, pf, pt, block_offset, fine_count)
    grad_features = lax.psum_scatter(
        fine_sum, "ch", scatter_dimension=0, tiled=True
    ).astype(BF16)
    factor = math.sqrt(offsets_all / (blocks * LANES * owners))
    grad_kernel = (lax.psum(weight_sum, "vox") * factor).astype(BF16)
    return (activation, grad_features, grad_kernel)


def solution(mesh):
    in_specs = (
        P("vox", None),
        P(None, "ch", None),
        P("ch", "vox"),
        P("vox"),
        P("vox"),
        P("vox"),
        P("vox", None),
        P("vox"),
        P("vox"),
    )
    out_specs = (P("ch", "vox"), P("ch", "vox"), P(None, "ch", None))
    return jax.shard_map(body, mesh=mesh, in_specs=in_specs, out_specs=out_specs, check_vma=False)
```

time: 236 us -> 144 us (0.61)
  other arithmetic: 64 us -> 3.6 us
  local copies, waits for them, and re-layouts: 55.7 us -> 4.16 us
  Pallas kernels: 0 us -> 21 us
  blocking collectives: 0 us -> 9.86 us
  waiting for transfers between devices: 86.5 us -> 80.9 us
  starting transfers between devices: 11 us -> 7.5 us
    scatter-add x7 -> x0, other arithmetic: 55.3 us -> none  [the longest x2 23.4 us: reverse_update(): fine_sum.at[fine_at.reshape(-1)].add(grad_in.reshape(-1, width_in))]
    gather x12 -> x0, local copies, waits for them, and re-layouts: 46.8 us -> none  [the longest x2 12.4 us: reverse_update(): grad_rows = grad_target[target_at]]
    pallas_call x0 -> x3, Pallas kernels: none -> 21 us  [the longest x1 9.15 us: body(): pl.pallas_call(functools.partial(backward_kernel, count), out_shape=(jax....]
    all_to_all x0 -> x1, blocking collectives: none -> 9.86 us  [body(): ret = lax.all_to_all(back, 'vox', split_axis=0, concat_axis=0, tiled=True)]
    all_to_all x2 -> x1, waiting for transfers between devices: 13.9 us -> 7.21 us  [body(): recv = lax.all_to_all(send, 'vox', split_axis=0, concat_axis=0, tiled=True)]
    all_to_all x2 -> x1, starting transfers between devices: 10.8 us -> 7.42 us  [body(): recv = lax.all_to_all(send, 'vox', split_axis=0, concat_axis=0, tiled=True)]
    while x9 -> x0, local copies, waits for them, and re-layouts: 2.81 us -> none
  transfers between devices with their start and end apart: 4 -> 3, of which waited for: 3 -> 2; matrix products, arithmetic and copies ran while one was open for 1% -> 1% of each run, Pallas kernels for 0% -> 0%
where the time goes in v1:
time: 144 us; the launch traced here: 143 us
  waiting for transfers between devices  80.9 us (56%)
  Pallas kernels  21 us (15%)
  between operations  16.2 us (11%)
  blocking collectives  9.86 us (7%)
  starting transfers between devices  7.5 us (5%)
  local copies, waits for them, and re-layouts  4.16 us (3%)
  other arithmetic  3.6 us (2%)
    psum x1, waiting for transfers between devices, body(): grad_kernel = (lax.psum(weight_sum, 'vox') * factor).astype(BF16)  73.2 us
    all_to_all x1, blocking collectives, body(): ret = lax.all_to_all(back, 'vox', split_axis=0, concat_axis=0, tiled=True)  9.86 us
    pallas_call x1, Pallas kernels, body(): pl.pallas_call(functools.partial(backward_kernel, count), out_shape=(jax....  9.15 us
    pallas_call x1, Pallas kernels, body(): pl.pallas_call(functools.partial(forward_kernel, count), out_shape=(excha...  8.62 us
    all_to_all x1, starting transfers between devices, body(): recv = lax.all_to_all(send, 'vox', split_axis=0, concat_axis=0, tiled=True)  7.42 us
    all_to_all x1, waiting for transfers between devices, body(): recv = lax.all_to_all(send, 'vox', split_axis=0, concat_axis=0, tiled=True)  7.21 us
    unnamed x22, local copies, waits for them, and re-layouts  4.08 us
    pallas_call x1, Pallas kernels, body(): pl.pallas_call(middle_kernel, out_shape=(jax.ShapeDtypeStruct((width_out,...  3.23 us
  transfers between devices with their start and end apart: 3, of which 2 were waited for; matrix products, arithmetic and copies ran while one was open for 1% of the time, Pallas kernels for 0%

profile of v1, /device:TPU:0, one launch (start us, length us, event | category | flops | bytes accessed | tf_op | source)
XLA Modules:
  0.0 143.2 jit_solution(11325906144073396290)
XLA Ops:
  8.6 0.0 copy-start.8
  8.7 0.0 copy-start.9
  8.7 0.7 copy-done.8
  9.3 0.0 copy-done.9
  9.3 0.0 copy-start
  9.3 1.0 copy-done
  10.3 0.0 copy-start.2
  10.3 0.9 copy-done.2
  11.3 0.0 copy-start.3
  11.3 0.7 copy-done.3
  12.0 0.0 copy-start.5
  12.0 0.7 copy-done.5
  12.7 0.0 copy-start.10
  12.7 8.6 %shard_map.112 = (bf16[8,64,128]{2,1,0:T(8,128)(2,1)}, s32[1,512]{1,0:T(1,128)S(1)}, bf16[8,128,512]{2,1,0:T(8,128)(2,1)S(1)}) custom-call(bf16[1024,128]{1,0:T(8,128)(2,1)S(1)} %copy-done.2, bf16[27,64,128]{2,1,0:T(8,128)(2,1)S(1)} %copy-done, s32[32,128]{1,0:T(8,128)S(1)} %bitcast.3, s32[32,128]{1,0:T(8,128)S(1)} %bitcast.5, s32[32]{0:T(128)S(1)} %copy-done.9, ...), custom_call_target="tpu_custom_call" | custom-call | tf_op jit(solution)/shard_map/pallas_call | solution.py:180
  21.4 7.4 %all-to-all-start = ((bf16[8,64,128]{2,1,0:T(8,128)(2,1)}), bf16[8,64,128]{2,1,0:T(8,128)(2,1)S(1)}, u32[]{:S(2)}, u32[]{:S(2)}) async-start(bf16[8,64,128]{2,1,0:T(8,128)(2,1)} %get-tuple-element.10), calls=%async_computation | async-start | bytes 262144 | tf_op jit(solution)/shard_map/all_to_all | solution.py:192
  28.8 0.0 all-reduce.3.cloned.1.call-start
  28.8 0.0 copy-done.10
  28.8 0.1 reshape.21
  28.9 7.2 %all-to-all-done.recv = bf16[8,64,128]{2,1,0:T(8,128)(2,1)S(1)} async-done(((bf16[8,64,128]{2,1,0:T(8,128)(2,1)}), bf16[8,64,128]{2,1,0:T(8,128)(2,1)S(1)}, u32[]{:S(2)}, u32[]{:S(2)}) %all-to-all-start) | async-done | bytes 131104 | tf_op jit(solution)/shard_map/all_to_all | solution.py:192
  36.1 0.0 copy-done.7
  36.1 3.2 %shard_map.113 = (bf16[64,512]{1,0:T(8,128)(2,1)}, bf16[8,64,128]{2,1,0:T(8,128)(2,1)S(1)}) custom-call(bf16[8,64,128]{2,1,0:T(8,128)(2,1)S(1)} %all-to-all-done.recv, s32[8,128]{1,0:T(8,128)S(1)} %pad.4.slots, bf16[64,512]{1,0:T(8,128)(2,1)S(1)} %copy-done.7), custom_call_target="tpu_custom_call" | custom-call | tf_op jit(solution)/shard_map/pallas_call | solution.py:193
  39.4 9.9 %all_to_all.10.ret = bf16[8,64,128]{2,1,0:T(8,128)(2,1)S(1)} all-to-all(bf16[8,64,128]{2,1,0:T(8,128)(2,1)S(1)} %get-tuple-element.12), channel_id=1, replica_groups=mesh['vox'=8,'ch'=4] {'vox'}, dimensions={0} | all-to-all | bytes 262144 | tf_op jit(solution)/shard_map/all_to_all | solution.py:200
  49.2 0.0 copy-done.1
  49.2 0.0 copy-done.4
  49.2 0.0 copy-done.6
  49.2 9.1 %shard_map.114 = (f32[128,1024]{1,0:T(8,128)}, f32[27,64,128]{2,1,0:T(8,128)}) custom-call(bf16[8,64,128]{2,1,0:T(8,128)(2,1)S(1)} %all_to_all.10.ret, s32[1,512]{1,0:T(1,128)S(1)} %get-tuple-element.13.slot, bf16[8,128,512]{2,1,0:T(8,128)(2,1)S(1)} %get-tuple-element.14.g_in, bf16[27,64,128]{2,1,0:T(8,128)(2,1)S(1)} %copy-done.1, s32[32,128]{1,0:T(8,128)S(1)} %bitcast.4, ...), custom_call_target="tpu_custom_call" | custom-call | tf_op jit(solution)/shard_map/pallas_call | solution.py:201
  58.4 0.0 all-reduce.3.cloned.1.call-update
  58.4 0.0 reduce-scatter.2.cloned.1.call-start
  58.4 0.5 reduce-scatter.2.cloned.1.call-update
  59.0 73.2 %all-reduce.3.cloned.1.call-done = f32[27,64,128]{2,1,0:T(8,128)} async-done(((f32[27,64,128]{2,1,0:T(8,128)}), f32[27,64,128]{2,1,0:T(8,128)}) %all-reduce.3.cloned.1.call-update) | async-done | bytes 884752 | tf_op jit(solution)/shard_map/psum | solution.py:216
  132.1 2.1 %multiply_convert_fusion = bf16[27,64,128]{2,1,0:T(8,128)(2,1)} fusion(f32[27,64,128]{2,1,0:T(8,128)} %all-reduce.3.cloned.1.call-done), kind=kLoop, calls=%fused_computation | loop fusion | flops 442368 | bytes 1327104 | tf_op jit(solution)/shard_map/convert_element_type | solution.py:216
  134.2 1.5 %convert_element_type.6 = bf16[32,1024]{1,0:T(8,128)(2,1)} convert(f32[32,1024]{1,0:T(8,128)} %reduce-scatter.2.cloned.1.call-done) | non-fusion elementwise | flops 32768 | bytes 196608 | tf_op jit(solution)/shard_map/convert_element_type | solution.py:214
  (6 shorter events, 0.0 us)
Async XLA Ops:
  8.6 0.7 copy-start.8
  8.7 0.7 copy-start.9
  9.3 1.0 copy-start
  10.3 0.9 copy-start.2
  11.3 0.7 copy-start.3
  12.0 0.7 copy-start.5
  12.7 16.1 %copy-start.10 = (s32[768]{0:T(1024)S(1)}, s32[768]{0:T(1024)}, u32[]{:S(2)}) copy-start(s32[768]{0:T(1024)} %param.16) | copy-start | bytes 9220
  12.7 23.4 %copy-start.7 = (bf16[64,512]{1,0:T(8,128)(2,1)S(1)}, bf16[64,512]{1,0:T(8,128)(2,1)}, u32[]{:S(2)}) copy-start(bf16[64,512]{1,0:T(8,128)(2,1)} %cg.1) | copy-start | bytes 196612
  21.4 27.9 %copy-start.1 = (bf16[27,64,128]{2,1,0:T(8,128)(2,1)S(1)}, bf16[27,64,128]{2,1,0:T(8,128)(2,1)}, u32[]{:S(2)}) copy-start(bf16[27,64,128]{2,1,0:T(8,128)(2,1)} %ker.3) | copy-start | bytes 1327108
  21.4 14.8 %all-to-all-start = ((bf16[8,64,128]{2,1,0:T(8,128)(2,1)}), bf16[8,64,128]{2,1,0:T(8,128)(2,1)S(1)}, u32[]{:S(2)}, u32[]{:S(2)}) async-start(bf16[8,64,128]{2,1,0:T(8,128)(2,1)} %get-tuple-element.10), calls=%async_computation | async-start | bytes 262144 | tf_op jit(solution)/shard_map/all_to_all | solution.py:192
  28.8 103.4 %all-reduce.3.cloned.1.call-start = ((), (), s32[]{:S(2)}) async-start(), calls=%async_computation.4 | async-start | bytes 1769472 | tf_op jit(solution)/shard_map/psum | solution.py:216
  39.3 9.9 %copy-start.4 = (s32[4096]{0:T(1024)S(1)}, s32[4096]{0:T(1024)}, u32[]{:S(2)}) copy-start(s32[4096]{0:T(1024)} %param.12) | copy-start | bytes 49156
  39.3 9.9 %copy-start.6 = (s32[4096]{0:T(1024)S(1)}, s32[4096]{0:T(1024)}, u32[]{:S(2)}) copy-start(s32[4096]{0:T(1024)} %param.13) | copy-start | bytes 49156
  58.4 75.8 %reduce-scatter.2.cloned.1.call-start = ((), (), s32[]{:S(2)}) async-start(), calls=%async_computation.3 | async-start | bytes 655360 | tf_op jit(solution)/shard_map/reduce_scatter | solution.py:212
Sparse Core Ops, SparseCore 0:
  58.5 73.5 all-reduce.2
Sparse Core Ops, SparseCore 1:
  61.3 19.3 reduce-scatter.1

commit v2 on v1

v2 whole, which is shorter than its diff:
```python
import functools
import math

import jax
import jax.numpy as jnp
from jax import lax
from jax.experimental import pallas as pl
from jax.experimental.pallas import tpu as pltpu
from jax.sharding import PartitionSpec as P

LANES = 128
MESH = pl.DeviceIdType.MESH
NT = (((1,), (1,)), ((), ()))
TN = (((0,), (0,)), ((), ()))
F32 = jnp.float32
BF16 = jnp.bfloat16


def dot(a, b, dims=(((1,), (0,)), ((), ()))):
    return lax.dot_general(a, b, dims, preferred_element_type=F32)


def onehot(rows, ids, base=0):
    at = lax.broadcasted_iota(jnp.int32, (rows, ids.shape[1]), 0) + base
    return (at == ids).astype(BF16)


def onehot_rows(rows, ids_ref, first, count):
    return jnp.concatenate(
        [onehot(rows, ids_ref[pl.ds(first + j, 1), :]) for j in range(count)], axis=1
    )


def split(value):
    high = value.astype(BF16)
    low = (value - high.astype(F32)).astype(BF16)
    return jnp.concatenate([high, low], axis=0)


def joined(value):
    half = value.shape[0] // 2
    return value[:half] + value[half:]


def slots_of(owner_row, owners, padded):
    targets = owner_row.shape[1]
    lead = max(owners, 8)
    mine = onehot(lead, owner_row)
    earlier = lax.broadcasted_iota(jnp.int32, (targets, targets), 0)
    later = lax.broadcasted_iota(jnp.int32, (targets, targets), 1)
    before = dot(mine, (earlier < later).astype(BF16))
    rank = jnp.sum(before * mine.astype(F32), axis=0, keepdims=True)
    return owner_row * padded + rank.astype(jnp.int32)


def whole_kernel(
    count,
    owners,
    channels,
    factor,
    off,
    live,
    feat_in,
    ker_in,
    cg_in,
    pf_in,
    pt_in,
    own_in,
    slots_in,
    act,
    fine_out,
    weight_out,
    feat,
    ker,
    cg,
    pf,
    pt,
    own,
    slots,
    ft,
    foh,
    toh,
    gath,
    spread,
    send,
    recv,
    back,
    ret,
    prefix,
    links,
    acc,
    fsum,
    fsend,
    frecv,
    wsum,
    wnear,
    wpass,
    wfar,
    wfin,
    in_sem,
    a_send,
    a_recv,
    b_send,
    b_recv,
    f_send,
    f_recv,
    near_send,
    near_recv,
    far_send,
    far_recv,
    out_send,
    out_recv,
    fwd_send,
    fwd_recv,
):
    fine_total, width_in = feat.shape
    offsets_all, width_out, _ = ker.shape
    targets = own.shape[1]
    coarse_total = cg.shape[1]
    padded = send.shape[2]
    blocks = pf.shape[0]
    groups = blocks // count
    slice_rows = wnear.shape[1]
    outer = owners // 2
    vox = lax.axis_index("vox")
    ch = lax.axis_index("ch")
    mine_out, mine_in = vox // 2, lax.rem(vox, 2)

    barrier = pltpu.get_barrier_semaphore()
    for step in range(1, owners):
        pl.semaphore_signal(
            barrier, inc=1, device_id=(lax.rem(vox + step, owners), ch), device_id_type=MESH
        )
    for step in range(1, channels):
        pl.semaphore_signal(
            barrier, inc=1, device_id=(vox, lax.rem(ch + step, channels)), device_id_type=MESH
        )

    pairs = [
        (pf_in, pf),
        (feat_in, feat),
        (pt_in, pt),
        (ker_in, ker),
        (own_in, own),
        (slots_in, slots),
        (cg_in, cg),
    ]
    loads = [pltpu.make_async_copy(a, b, in_sem.at[i]) for i, (a, b) in enumerate(pairs)]
    for load in loads:
        load.start()
    for load in loads[:4]:
        load.wait()

    at = lax.broadcasted_iota(jnp.int32, (fine_total, width_in), 0)
    ft[...] = jnp.where(at < live[0], feat[...].astype(F32), 0.0).T.astype(BF16)

    def forward(g, total):
        foh[g] = onehot_rows(fine_total, pf, g * count, count)
        gathered = dot(ft[...], foh[g]).astype(BF16)
        gath[g] = gathered
        part = jnp.concatenate(
            [
                dot(ker[off[g * count + j]], gathered[:, j * LANES : (j + 1) * LANES])
                for j in range(count)
            ],
            axis=1,
        )
        toh[g] = onehot_rows(targets, pt, g * count, count)
        return total + dot(split(part), toh[g], NT)

    total = lax.fori_loop(0, groups, forward, jnp.zeros((2 * width_out, targets), F32))
    part = joined(total).astype(BF16)
    for load in loads[4:]:
        load.wait()
    slot = slots_of(own[...], owners, padded)

    def route(o, carry):
        send[o] = dot(part, onehot(padded, slot, o * padded), NT).astype(BF16)
        return carry

    lax.fori_loop(0, owners, route, 0, unroll=owners <= 8)

    def exchange(source, target, out_sem, in_sem_of):
        copies = []
        for step in range(1, owners):
            to = lax.rem(vox + step, owners)
            copies.append(
                pltpu.make_async_remote_copy(
                    src_ref=source.at[to],
                    dst_ref=target.at[vox],
                    send_sem=out_sem.at[step],
                    recv_sem=in_sem_of.at[step],
                    device_id=(to, ch),
                    device_id_type=MESH,
                )
            )
            copies[-1].start()
        target[vox] = source[vox]
        return copies

    pl.semaphore_wait(barrier, owners - 1 + channels - 1)
    copies = exchange(send, recv, a_send, a_recv)

    def link(b, carry):
        found = jnp.int32(0)
        for other in range(blocks):
            same = jnp.logical_and(off[other] == off[b], other < b)
            found = jnp.where(same, jnp.int32(other + 1), found)
        links[b] = found
        return carry

    def ending(k, carry):
        found = jnp.int32(0)
        for other in range(blocks):
            found = jnp.where(off[other] == k, jnp.int32(other + 1), found)
        links[blocks + k] = found
        return carry

    lax.fori_loop(0, blocks, link, 0)
    lax.fori_loop(0, offsets_all, ending, 0)
    for copy in copies:
        copy.wait()

    def gather(o, total):
        return total + dot(recv[o], onehot(coarse_total, slots[pl.ds(o, 1), :]), NT)

    coarse = lax.fori_loop(
        0, owners, gather, jnp.zeros((width_out, coarse_total), F32), unroll=owners <= 8
    )
    gate = jax.nn.sigmoid(coarse)
    act[...] = (coarse * gate).astype(BF16)
    grad = (cg[...].astype(F32) * gate * (1.0 + coarse * (1.0 - gate))).astype(BF16)

    def give(o, carry):
        back[o] = dot(grad, onehot(coarse_total, slots[pl.ds(o, 1), :])).astype(BF16)
        return carry

    lax.fori_loop(0, owners, give, 0, unroll=owners <= 8)
    copies = exchange(back, ret, b_send, b_recv)
    acc[...] = jnp.zeros_like(acc)
    prefix[0] = jnp.zeros_like(prefix[0])
    wsum[...] = jnp.zeros_like(wsum)
    for copy in copies:
        copy.wait()

    def take(o, total):
        return total + dot(ret[o], onehot(padded, slot, o * padded))

    grad = lax.fori_loop(
        0, owners, take, jnp.zeros((width_out, targets), F32), unroll=owners <= 8
    ).astype(BF16)

    def weigh(g, carry):
        rows = dot(grad, toh[g]).astype(BF16)
        spread[g] = rows
        gathered = gath[g]
        for j in range(count):
            lanes = slice(j * LANES, (j + 1) * LANES)
            b = g * count + j
            prefix[b + 1] = prefix[links[b]] + dot(rows[:, lanes], gathered[:, lanes], NT)
        return carry

    lax.fori_loop(0, groups, weigh, 0)

    def pick(k, carry):
        rows = pl.ds(pl.multiple_of(k * width_out, width_out), width_out)
        wsum[rows, :] = prefix[links[blocks + k]].astype(BF16)
        return carry

    lax.fori_loop(0, offsets_all, pick, 0)

    def slice_of(out_at, in_at):
        first = (out_at * 2 + in_at) * slice_rows
        return pl.ds(pl.multiple_of(first, 16), slice_rows)

    partner = mine_out * 2 + 1 - mine_in
    order = list(range(1, outer)) + [0]
    near = {}
    for step in order:
        to = lax.rem(mine_out + step, outer)
        near[step] = pltpu.make_async_remote_copy(
            src_ref=wsum.at[slice_of(to, 1 - mine_in)],
            dst_ref=wnear.at[step],
            send_sem=near_send.at[step],
            recv_sem=near_recv.at[step],
            device_id=(partner, ch),
            device_id_type=MESH,
        )
        near[step].start()

    def scatter(g, carry):
        parts = []
        for j in range(count):
            k = off[g * count + j]
            parts.append(dot(ker[k], spread[g, :, j * LANES : (j + 1) * LANES], TN))
        acc[...] += dot(split(jnp.concatenate(parts, axis=1)), foh[g], NT)
        return carry

    far = {}
    done = 0
    for number, step in enumerate(order):
        until = groups * (number + 1) // outer
        if until > done:
            lax.fori_loop(done, until, scatter, 0)
            done = until
        to = lax.rem(mine_out + step, outer)
        near[step].wait()
        both = wsum[slice_of(to, mine_in), :].astype(F32) + wnear[step].astype(F32)
        if step == 0:
            total = both
        else:
            wpass[step] = both.astype(BF16)
            far[step] = pltpu.make_async_remote_copy(
                src_ref=wpass.at[step],
                dst_ref=wfar.at[step],
                send_sem=far_send.at[step],
                recv_sem=far_recv.at[step],
                device_id=(to * 2 + mine_in, ch),
                device_id_type=MESH,
            )
            far[step].start()

    share = width_in // channels
    mask_at = lax.broadcasted_iota(jnp.int32, (width_in, fine_total), 1)
    whole = jnp.where(mask_at < live[0], joined(acc[...]), 0.0)
    fsum[...] = whole
    fsend[...] = whole.astype(BF16)
    fine = []
    for step in range(1, channels):
        to = lax.rem(ch + step, channels)
        fine.append(
            pltpu.make_async_remote_copy(
                src_ref=fsend.at[pl.ds(pl.multiple_of(to * share, share), share)],
                dst_ref=frecv.at[step],
                send_sem=f_send.at[step],
                recv_sem=f_recv.at[step],
                device_id=(vox, to),
                device_id_type=MESH,
            )
        )
        fine[-1].start()

    for step in order[:-1]:
        far[step].wait()
        total = total + wfar[step].astype(F32)
    here = slice_of(mine_out, mine_in)
    wfin[here, :] = (total * factor).astype(BF16)

    def finished(where, to, out_sem, in_sem_of):
        copy = pltpu.make_async_remote_copy(
            src_ref=wfin.at[where],
            dst_ref=wfin.at[where],
            send_sem=out_sem,
            recv_sem=in_sem_of,
            device_id=(to, ch),
            device_id_type=MESH,
        )
        copy.start()
        return copy

    outward = [
        finished(
            here,
            lax.rem(mine_out + step, outer) * 2 + mine_in,
            out_send.at[step],
            out_recv.at[step],
        )
        for step in range(1, outer)
    ]
    across = [finished(here, partner, fwd_send.at[0], fwd_recv.at[0])]

    for copy in fine:
        copy.wait()
    kept = fsum[pl.ds(pl.multiple_of(ch * share, share), share), :]
    for step in range(1, channels):
        kept = kept + frecv[step].astype(F32)
    fine_out[...] = kept.astype(BF16)

    for step in range(1, outer):
        outward[step - 1].wait()
        came = slice_of(lax.rem(mine_out + outer - step, outer), mine_in)
        across.append(finished(came, partner, fwd_send.at[step], fwd_recv.at[step]))
    for copy in across:
        copy.wait()

    def deliver(k, carry):
        rows = pl.ds(pl.multiple_of(k * width_out, width_out), width_out)
        weight_out[k] = wfin[rows, :]
        return carry

    lax.fori_loop(0, offsets_all, deliver, 0)


def body(
    features,
    kernel,
    coarse_grad,
    pair_fine,
    pair_target,
    block_offset,
    target_owner,
    slot_coarse_row,
    fine_count,
):
    owners = lax.axis_size("vox")
    channels = lax.axis_size("ch")
    fine_total, width_in = features.shape
    width_out, coarse_total = coarse_grad.shape
    offsets_all = kernel.shape[0]
    targets = target_owner.shape[0]
    capacity = slot_coarse_row.shape[0] // owners
    blocks = block_offset.shape[0]
    padded = -(-capacity // LANES) * LANES
    count = 4
    groups = blocks // count
    outer = owners // 2
    slice_rows = -(-offsets_all * width_out // (owners * 16)) * 16
    share = width_in // channels
    vm = pl.BlockSpec(memory_space=pltpu.VMEM)
    sm = pl.BlockSpec(memory_space=pltpu.SMEM)
    hbm = pl.BlockSpec(memory_space=pl.ANY)
    pf = pair_fine.reshape(blocks, LANES)
    pt = pair_target.reshape(blocks, LANES)
    own = target_owner.reshape(1, targets)
    slots = jnp.pad(
        slot_coarse_row.reshape(owners, capacity),
        ((0, 0), (0, padded - capacity)),
        constant_values=-1,
    )
    factor = math.sqrt(offsets_all / (blocks * LANES * owners))
    operands = (features, kernel, coarse_grad, pf, pt, own, slots)
    wide = count * LANES
    dma = pltpu.SemaphoreType.DMA
    scratch = [pltpu.VMEM(a.shape, a.dtype) for a in operands] + [
        pltpu.VMEM((width_in, fine_total), BF16),
        pltpu.VMEM((groups, fine_total, wide), BF16),
        pltpu.VMEM((groups, targets, wide), BF16),
        pltpu.VMEM((groups, width_in, wide), BF16),
        pltpu.VMEM((groups, width_out, wide), BF16),
        pltpu.VMEM((owners, width_out, padded), BF16),
        pltpu.VMEM((owners, width_out, padded), BF16),
        pltpu.VMEM((owners, width_out, padded), BF16),
        pltpu.VMEM((owners, width_out, padded), BF16),
        pltpu.VMEM((blocks + 1, width_out, width_in), F32),
        pltpu.SMEM((blocks + offsets_all,), jnp.int32),
        pltpu.VMEM((2 * width_in, fine_total), F32),
        pltpu.VMEM((width_in, fine_total), F32),
        pltpu.VMEM((width_in, fine_total), BF16),
        pltpu.VMEM((channels, share, fine_total), BF16),
        pltpu.VMEM((owners * slice_rows, width_in), BF16),
        pltpu.VMEM((outer, slice_rows, width_in), BF16),
        pltpu.VMEM((outer, slice_rows, width_in), BF16),
        pltpu.VMEM((outer, slice_rows, width_in), BF16),
        pltpu.VMEM((owners * slice_rows, width_in), BF16),
        dma((len(operands),)),
        dma((owners,)),
        dma((owners,)),
        dma((owners,)),
        dma((owners,)),
        dma((channels,)),
        dma((channels,)),
    ] + [dma((outer,)) for _ in range(8)]
    return pl.pallas_call(
        functools.partial(whole_kernel, count, owners, channels, factor),
        out_shape=(
            jax.ShapeDtypeStruct((width_out, coarse_total), BF16),
            jax.ShapeDtypeStruct((share, fine_total), BF16),
            jax.ShapeDtypeStruct(kernel.shape, BF16),
        ),
        in_specs=[sm, sm] + [hbm] * len(operands),
        out_specs=(vm, vm, vm),
        scratch_shapes=scratch,
        compiler_params=pltpu.CompilerParams(
            collective_id=0, has_side_effects=True, vmem_limit_bytes=50 * 2**20
        ),
    )(block_offset, fine_count, *operands)


def solution(mesh):
    in_specs = (
        P("vox", None),
        P(None, "ch", None),
        P("ch", "vox"),
        P("vox"),
        P("vox"),
        P("vox"),
        P("vox", None),
        P("vox"),
        P("vox"),
    )
    out_specs = (P("ch", "vox"), P("ch", "vox"), P(None, "ch", None))
    return jax.shard_map(body, mesh=mesh, in_specs=in_specs, out_specs=out_specs, check_vma=False)
```

time: 144 us -> 53 us (0.37)
  waiting for transfers between devices: 80.9 us -> 0 us
  Pallas kernels: 21 us -> 45 us
  between operations: 16.2 us -> 1.34 us
  blocking collectives: 9.86 us -> 0 us
  starting transfers between devices: 7.5 us -> 0 us
  other arithmetic: 3.6 us -> 0 us
  local copies, waits for them, and re-layouts: 4.16 us -> 6.3 us
    psum x1 -> x0, waiting for transfers between devices: 73.2 us -> none  [body(): grad_kernel = (lax.psum(weight_sum, 'vox') * factor).astype(BF16)]
    pallas_call x3 -> x1, Pallas kernels: 21 us -> 45 us  [body(): pl.pallas_call(functools.partial(whole_kernel, count, owners, channels, f...]
    all_to_all x1 -> x0, blocking collectives: 9.86 us -> none  [body(): ret = lax.all_to_all(back, 'vox', split_axis=0, concat_axis=0, tiled=True)]
    all_to_all x1 -> x0, starting transfers between devices: 7.42 us -> none  [body(): recv = lax.all_to_all(send, 'vox', split_axis=0, concat_axis=0, tiled=True)]
    all_to_all x1 -> x0, waiting for transfers between devices: 7.21 us -> none  [body(): recv = lax.all_to_all(send, 'vox', split_axis=0, concat_axis=0, tiled=True)]
    convert_element_type x2 -> x0, other arithmetic: 3.6 us -> none  [the longest x1 2.06 us: body(): grad_kernel = (lax.psum(weight_sum, 'vox') * factor).astype(BF16)]
    unnamed x22 -> x19, local copies, waits for them, and re-layouts: 4.08 us -> 6.22 us
  transfers between devices with their start and end apart: 3 -> 0, of which waited for: 2 -> 0; matrix products, arithmetic and copies ran while one was open for 1% -> 0% of each run, Pallas kernels for 0% -> 0%
where the time goes in v2:
time: 53 us; the launch traced here: 52.7 us
  Pallas kernels  45 us (85%)
  local copies, waits for them, and re-layouts  6.3 us (12%)
  between operations  1.34 us (3%)
    pallas_call x1, Pallas kernels, body(): pl.pallas_call(functools.partial(whole_kernel, count, owners, channels, f...  45 us
    unnamed x19, local copies, waits for them, and re-layouts  6.22 us

profile of v2, /device:TPU:0, one launch (start us, length us, event | category | flops | bytes accessed | tf_op | source)
XLA Modules:
  0.0 52.7 jit_solution(15636251545175959232)
XLA Ops:
  0.6 0.0 copy-start.7
  0.6 0.0 copy-start.3
  1.3 0.0 copy-done.7
  1.3 0.1 reshape.21
  1.4 0.0 copy-start.5
  1.4 0.0 copy-start.6
  1.4 0.0 copy-done.3
  1.4 0.7 %copy-done.5 = s32[512,1]{0,1:T(1,128)S(1)} copy-done((s32[512,1]{0,1:T(1,128)S(1)}, s32[512,1]{0,1:T(1,128)}, u32[]{:S(2)}) %copy-start.5) | copy-done | bytes 2072
  2.1 0.0 copy-done.6
  2.1 0.0 copy-start
  2.1 1.0 %copy-done = bf16[27,64,128]{2,1,0:T(8,128)(2,1)S(1)} copy-done((bf16[27,64,128]{2,1,0:T(8,128)(2,1)S(1)}, bf16[27,64,128]{2,1,0:T(8,128)(2,1)}, u32[]{:S(2)}) %copy-start) | copy-done | bytes 442392
  3.1 0.0 copy-start.1
  3.1 0.9 %copy-done.1 = bf16[1024,128]{1,0:T(8,128)(2,1)S(1)} copy-done((bf16[1024,128]{1,0:T(8,128)(2,1)S(1)}, bf16[1024,128]{1,0:T(8,128)(2,1)}, u32[]{:S(2)}) %copy-start.1) | copy-done | bytes 262168
  4.0 0.0 copy-start.2
  4.0 0.8 %copy-done.2 = bf16[64,512]{1,0:T(8,128)(2,1)S(1)} copy-done((bf16[64,512]{1,0:T(8,128)(2,1)S(1)}, bf16[64,512]{1,0:T(8,128)(2,1)}, u32[]{:S(2)}) %copy-start.2) | copy-done | bytes 65560
  4.9 0.0 copy-start.4
  4.9 0.7 %copy-done.4 = s32[4096]{0:T(1024)S(1)} copy-done((s32[4096]{0:T(1024)S(1)}, s32[4096]{0:T(1024)}, u32[]{:S(2)}) %copy-start.4) | copy-done | bytes 16408
  5.6 45.0 %shard_map.112 = (bf16[64,512]{1,0:T(8,128)(2,1)S(1)}, bf16[32,1024]{1,0:T(8,128)(2,1)S(1)}, bf16[27,64,128]{2,1,0:T(8,128)(2,1)S(1)}) custom-call(s32[32]{0:T(128)S(1)} %copy-done.6, s32[1]{0:T(128)S(6)} %copy.15.live, bf16[1024,128]{1,0:T(8,128)(2,1)S(1)} %copy-done.1, bf16[27,64,128]{2,1,0:T(8,128)(2,1)S(1)} %copy-done, bf16[64,512]{1,0:T(8,128)(2,1)S(1)} %copy-done.2, ...), custom_call_target="tpu_custom_call" | custom-call | tf_op jit(solution)/shard_map/pallas_call | solution.py:463
  50.7 0.6 %copy.16 = bf16[64,512]{1,0:T(8,128)(2,1)} copy(bf16[64,512]{1,0:T(8,128)(2,1)S(1)} %get-tuple-element.6) | data formatting | bytes 131072
  51.3 0.6 %copy.17 = bf16[32,1024]{1,0:T(8,128)(2,1)} copy(bf16[32,1024]{1,0:T(8,128)(2,1)S(1)} %get-tuple-element.7) | data formatting | bytes 131072
  51.9 0.8 %copy.18 = bf16[27,64,128]{2,1,0:T(8,128)(2,1)} copy(bf16[27,64,128]{2,1,0:T(8,128)(2,1)S(1)} %get-tuple-element.8) | data formatting | bytes 884736
  (1 shorter events, 0.0 us)
Async XLA Ops:
  0.6 0.7 %copy-start.7 = (s32[768]{0:T(1024)S(1)}, s32[768]{0:T(1024)}, u32[]{:S(2)}) copy-start(s32[768]{0:T(1024)} %param.16) | copy-start | bytes 9220
  0.6 0.8 %copy-start.3 = (s32[4096]{0:T(1024)S(1)}, s32[4096]{0:T(1024)}, u32[]{:S(2)}) copy-start(s32[4096]{0:T(1024)} %param.12) | copy-start | bytes 49156
  1.4 0.7 %copy-start.5 = (s32[512,1]{0,1:T(1,128)S(1)}, s32[512,1]{0,1:T(1,128)}, u32[]{:S(2)}) copy-start(s32[512,1]{0,1:T(1,128)} %param.15) | copy-start | bytes 6148
  1.4 0.7 %copy-start.6 = (s32[32]{0:T(128)S(1)}, s32[32]{0:T(128)}, u32[]{:S(2)}) copy-start(s32[32]{0:T(128)} %off.1) | copy-start | bytes 388
  2.1 1.0 %copy-start = (bf16[27,64,128]{2,1,0:T(8,128)(2,1)S(1)}, bf16[27,64,128]{2,1,0:T(8,128)(2,1)}, u32[]{:S(2)}) copy-start(bf16[27,64,128]{2,1,0:T(8,128)(2,1)} %ker_in.1) | copy-start | bytes 1327108
  3.1 0.9 %copy-start.1 = (bf16[1024,128]{1,0:T(8,128)(2,1)S(1)}, bf16[1024,128]{1,0:T(8,128)(2,1)}, u32[]{:S(2)}) copy-start(bf16[1024,128]{1,0:T(8,128)(2,1)} %feat_in.1) | copy-start | bytes 786436
  4.0 0.8 %copy-start.2 = (bf16[64,512]{1,0:T(8,128)(2,1)S(1)}, bf16[64,512]{1,0:T(8,128)(2,1)}, u32[]{:S(2)}) copy-start(bf16[64,512]{1,0:T(8,128)(2,1)} %cg_in.1) | copy-start | bytes 196612
  4.9 0.7 %copy-start.4 = (s32[4096]{0:T(1024)S(1)}, s32[4096]{0:T(1024)}, u32[]{:S(2)}) copy-start(s32[4096]{0:T(1024)} %param.13) | copy-start | bytes 49156

commit v3 on v2

--- a/solution.py
+++ b/solution.py
@@ -21,8 +21,10 @@
 
 
 def onehot(rows, ids, base=0):
-    at = lax.broadcasted_iota(jnp.int32, (rows, ids.shape[1]), 0) + base
-    return (at == ids).astype(BF16)
+    at = lax.broadcasted_iota(jnp.int32, (rows, ids.shape[1]), 0).astype(jnp.int16)
+    wanted = jnp.clip(ids - base, -1, rows).astype(jnp.int16)
+    one = jnp.ones(at.shape, BF16)
+    return jnp.where(at == wanted, one, jnp.zeros_like(one))
 
 
 def onehot_rows(rows, ids_ref, first, count):
@@ -67,9 +69,11 @@
     pt_in,
     own_in,
     slots_in,
-    act,
+    act_out,
     fine_out,
     weight_out,
+    act,
+    fine_here,
     feat,
     ker,
     cg,
@@ -77,6 +81,8 @@
     pt,
     own,
     slots,
+    routes,
+    places,
     ft,
     foh,
     toh,
@@ -98,6 +104,7 @@
     wfar,
     wfin,
     in_sem,
+    end_sem,
     a_send,
     a_recv,
     b_send,
@@ -137,18 +144,37 @@
         )
 
     pairs = [
-        (pf_in, pf),
-        (feat_in, feat),
-        (pt_in, pt),
-        (ker_in, ker),
         (own_in, own),
         (slots_in, slots),
+        (pf_in, pf),
+        (pt_in, pt),
+        (feat_in, feat),
+        (ker_in, ker),
         (cg_in, cg),
     ]
     loads = [pltpu.make_async_copy(a, b, in_sem.at[i]) for i, (a, b) in enumerate(pairs)]
     for load in loads:
         load.start()
-    for load in loads[:4]:
+    small = owners <= 16
+    for load in loads[:2]:
+        load.wait()
+    slot = slots_of(own[...], owners, padded)
+    if small:
+        routes[...] = onehot(owners * padded, slot)
+        capacity = slots.shape[0] * LANES // owners
+        blank = jnp.full((1, padded - capacity), -1, jnp.int32)
+        for o in range(owners):
+            pieces, first = [], o * capacity
+            while first < (o + 1) * capacity:
+                row, lane = divmod(first, LANES)
+                size = min(LANES - lane, (o + 1) * capacity - first)
+                pieces.append(slots[row : row + 1, lane : lane + size])
+                first += size
+            if padded > capacity:
+                pieces.append(blank)
+            ids = jnp.concatenate(pieces, axis=1)
+            places[:, o * padded : (o + 1) * padded] = onehot(coarse_total, ids)
+    for load in loads[2:6]:
         load.wait()
 
     at = lax.broadcasted_iota(jnp.int32, (fine_total, width_in), 0)
@@ -168,17 +194,27 @@
         toh[g] = onehot_rows(targets, pt, g * count, count)
         return total + dot(split(part), toh[g], NT)
 
-    total = lax.fori_loop(0, groups, forward, jnp.zeros((2 * width_out, targets), F32))
+    total = lax.fori_loop(
+        0, groups, forward, jnp.zeros((2 * width_out, targets), F32), unroll=True
+    )
     part = joined(total).astype(BF16)
-    for load in loads[4:]:
-        load.wait()
-    slot = slots_of(own[...], owners, padded)
 
     def route(o, carry):
         send[o] = dot(part, onehot(padded, slot, o * padded), NT).astype(BF16)
         return carry
 
-    lax.fori_loop(0, owners, route, 0, unroll=owners <= 8)
+    def apart(value, target):
+        for o in range(owners):
+            target[o] = value[:, o * padded : (o + 1) * padded].astype(BF16)
+
+    def together(source):
+        return jnp.concatenate([source[o] for o in range(owners)], axis=1)
+
+    if small:
+        apart(dot(part, routes[...], NT), send)
+    else:
+        lax.fori_loop(0, owners, route, 0)
+    loads[6].wait()
 
     def exchange(source, target, out_sem, in_sem_of):
         copies = []
@@ -224,18 +260,24 @@
     def gather(o, total):
         return total + dot(recv[o], onehot(coarse_total, slots[pl.ds(o, 1), :]), NT)
 
-    coarse = lax.fori_loop(
-        0, owners, gather, jnp.zeros((width_out, coarse_total), F32), unroll=owners <= 8
-    )
+    if small:
+        coarse = dot(together(recv), places[...], NT)
+    else:
+        coarse = lax.fori_loop(0, owners, gather, jnp.zeros(cg.shape, F32))
     gate = jax.nn.sigmoid(coarse)
     act[...] = (coarse * gate).astype(BF16)
+    stores = [pltpu.make_async_copy(act, act_out, end_sem.at[0])]
+    stores[-1].start()
     grad = (cg[...].astype(F32) * gate * (1.0 + coarse * (1.0 - gate))).astype(BF16)
 
     def give(o, carry):
         back[o] = dot(grad, onehot(coarse_total, slots[pl.ds(o, 1), :])).astype(BF16)
         return carry
 
-    lax.fori_loop(0, owners, give, 0, unroll=owners <= 8)
+    if small:
+        apart(dot(grad, places[...]), back)
+    else:
+        lax.fori_loop(0, owners, give, 0)
     copies = exchange(back, ret, b_send, b_recv)
     acc[...] = jnp.zeros_like(acc)
     prefix[0] = jnp.zeros_like(prefix[0])
@@ -246,9 +288,12 @@
     def take(o, total):
         return total + dot(ret[o], onehot(padded, slot, o * padded))
 
-    grad = lax.fori_loop(
-        0, owners, take, jnp.zeros((width_out, targets), F32), unroll=owners <= 8
-    ).astype(BF16)
+    if small:
+        grad = dot(together(ret), routes[...]).astype(BF16)
+    else:
+        grad = lax.fori_loop(
+            0, owners, take, jnp.zeros((width_out, targets), F32)
+        ).astype(BF16)
 
     def weigh(g, carry):
         rows = dot(grad, toh[g]).astype(BF16)
@@ -260,7 +305,7 @@
             prefix[b + 1] = prefix[links[b]] + dot(rows[:, lanes], gathered[:, lanes], NT)
         return carry
 
-    lax.fori_loop(0, groups, weigh, 0)
+    lax.fori_loop(0, groups, weigh, 0, unroll=True)
 
     def pick(k, carry):
         rows = pl.ds(pl.multiple_of(k * width_out, width_out), width_out)
@@ -301,7 +346,7 @@
     for number, step in enumerate(order):
         until = groups * (number + 1) // outer
         if until > done:
-            lax.fori_loop(done, until, scatter, 0)
+            lax.fori_loop(done, until, scatter, 0, unroll=True)
             done = until
         to = lax.rem(mine_out + step, outer)
         near[step].wait()
@@ -374,7 +419,9 @@
     kept = fsum[pl.ds(pl.multiple_of(ch * share, share), share), :]
     for step in range(1, channels):
         kept = kept + frecv[step].astype(F32)
-    fine_out[...] = kept.astype(BF16)
+    fine_here[...] = kept.astype(BF16)
+    stores.append(pltpu.make_async_copy(fine_here, fine_out, end_sem.at[1]))
+    stores[-1].start()
 
     for step in range(1, outer):
         outward[step - 1].wait()
@@ -383,12 +430,22 @@
     for copy in across:
         copy.wait()
 
-    def deliver(k, carry):
-        rows = pl.ds(pl.multiple_of(k * width_out, width_out), width_out)
-        weight_out[k] = wfin[rows, :]
-        return carry
-
-    lax.fori_loop(0, offsets_all, deliver, 0)
+    rows = offsets_all * width_out
+    stores.append(
+        pltpu.make_async_copy(wfin.at[pl.ds(0, rows)], weight_out, end_sem.at[2])
+    )
+    stores[-1].start()
+    for copy in stores:
+        copy.wait()
+
+
+def write_kernel(a, b, c, a_out, b_out, c_out, sem):
+    pairs = ((c, c_out), (a, a_out), (b, b_out))
+    copies = [pltpu.make_async_copy(x, y, sem.at[i]) for i, (x, y) in enumerate(pairs)]
+    for copy in copies:
+        copy.start()
+    for copy in copies:
+        copy.wait()
 
 
 def body(
@@ -416,22 +473,34 @@
     outer = owners // 2
     slice_rows = -(-offsets_all * width_out // (owners * 16)) * 16
     share = width_in // channels
-    vm = pl.BlockSpec(memory_space=pltpu.VMEM)
     sm = pl.BlockSpec(memory_space=pltpu.SMEM)
-    hbm = pl.BlockSpec(memory_space=pl.ANY)
+    hbm = pl.BlockSpec(memory_space=pltpu.HBM)
     pf = pair_fine.reshape(blocks, LANES)
     pt = pair_target.reshape(blocks, LANES)
     own = target_owner.reshape(1, targets)
-    slots = jnp.pad(
-        slot_coarse_row.reshape(owners, capacity),
-        ((0, 0), (0, padded - capacity)),
-        constant_values=-1,
-    )
+    small = owners <= 16
+    if small:
+        slots = slot_coarse_row.reshape(-1, LANES)
+    else:
+        slots = jnp.pad(
+            slot_coarse_row.reshape(owners, capacity),
+            ((0, 0), (0, padded - capacity)),
+            constant_values=-1,
+        )
+    kept = owners * padded if small else LANES
     factor = math.sqrt(offsets_all / (blocks * LANES * owners))
     operands = (features, kernel, coarse_grad, pf, pt, own, slots)
     wide = count * LANES
     dma = pltpu.SemaphoreType.DMA
-    scratch = [pltpu.VMEM(a.shape, a.dtype) for a in operands] + [
+    shapes = (
+        jax.ShapeDtypeStruct((width_out, coarse_total), BF16),
+        jax.ShapeDtypeStruct((share, fine_total), BF16),
+        jax.ShapeDtypeStruct(kernel.shape, BF16),
+    )
+    scratch = [pltpu.VMEM(a.shape, BF16) for a in shapes[:2]]
+    scratch += [pltpu.VMEM(a.shape, a.dtype) for a in operands] + [
+        pltpu.VMEM((kept, targets), BF16),
+        pltpu.VMEM((coarse_total, kept), BF16),
         pltpu.VMEM((width_in, fine_total), BF16),
         pltpu.VMEM((groups, fine_total, wide), BF16),
         pltpu.VMEM((groups, targets, wide), BF16),
@@ -453,6 +522,7 @@
         pltpu.VMEM((outer, slice_rows, width_in), BF16),
         pltpu.VMEM((owners * slice_rows, width_in), BF16),
         dma((len(operands),)),
+        dma((3,)),
         dma((owners,)),
         dma((owners,)),
         dma((owners,)),
@@ -460,20 +530,25 @@
         dma((channels,)),
         dma((channels,)),
     ] + [dma((outer,)) for _ in range(8)]
-    return pl.pallas_call(
+    results = pl.pallas_call(
         functools.partial(whole_kernel, count, owners, channels, factor),
-        out_shape=(
-            jax.ShapeDtypeStruct((width_out, coarse_total), BF16),
-            jax.ShapeDtypeStruct((share, fine_total), BF16),
-            jax.ShapeDtypeStruct(kernel.shape, BF16),
-        ),
+        out_shape=shapes[:2]
+        + (jax.ShapeDtypeStruct((offsets_all * width_out, width_in), BF16),),
         in_specs=[sm, sm] + [hbm] * len(operands),
-        out_specs=(vm, vm, vm),
+        out_specs=(hbm, hbm, hbm),
         scratch_shapes=scratch,
         compiler_params=pltpu.CompilerParams(
-            collective_id=0, has_side_effects=True, vmem_limit_bytes=50 * 2**20
+            collective_id=0, has_side_effects=True, vmem_limit_bytes=60 * 2**20
         ),
     )(block_offset, fine_count, *operands)
+    return pl.pallas_call(
+        write_kernel,
+        out_shape=shapes,
+        in_specs=[hbm, hbm, hbm],
+        out_specs=(hbm, hbm, hbm),
+        scratch_shapes=[dma((3,))],
+        compiler_params=pltpu.CompilerParams(vmem_limit_bytes=60 * 2**20),
+    )(results[0], results[1], results[2].reshape(kernel.shape))
 
 
 def solution(mesh):

time: 53 us -> 62.2 us (1.17)
  Pallas kernels: 45 us -> 60.8 us
  local copies, waits for them, and re-layouts: 6.3 us -> 0 us
    pallas_call x0 -> x1, Pallas kernels: none -> 18.5 us  [body(): pl.pallas_call(write_kernel, out_shape=shapes, in_specs=[hbm, hbm, hbm],...]
    unnamed x19 -> x0, local copies, waits for them, and re-layouts: 6.22 us -> none
    pallas_call x1, Pallas kernels: 45 us -> 42.3 us  [body(): pl.pallas_call(functools.partial(whole_kernel, count, owners, channels, f...]
where the time goes in v3:
time: 62.2 us; the launch traced here: 62.1 us
  Pallas kernels  60.8 us (98%)
  between operations  1.29 us (2%)
    pallas_call x1, Pallas kernels, body(): pl.pallas_call(functools.partial(whole_kernel, count, owners, channels, f...  42.3 us
    pallas_call x1, Pallas kernels, body(): pl.pallas_call(write_kernel, out_shape=shapes, in_specs=[hbm, hbm, hbm],...  18.5 us

profile of v3, /device:TPU:0, one launch (start us, length us, event | category | flops | bytes accessed | tf_op | source)
XLA Modules:
  0.0 62.1 jit_solution(3374560623996585498)
XLA Ops:
  1.3 42.3 %shard_map.112 = (bf16[64,512]{1,0:T(8,128)(2,1)}, bf16[32,1024]{1,0:T(8,128)(2,1)}, bf16[1728,128]{1,0:T(8,128)(2,1)}) custom-call(s32[32]{0:T(128)} %off.1, s32[1]{0:T(128)S(6)} %copy.12.live, bf16[1024,128]{1,0:T(8,128)(2,1)} %feat_in.1, bf16[27,64,128]{2,1,0:T(8,128)(2,1)} %ker_in.1, bf16[64,512]{1,0:T(8,128)(2,1)} %cg_in.1, s32[32,128]{1,0:T(8,128)} %bitcast.6, ...), custom_call_target="tpu_custom_call" | custom-call | tf_op jit(solution)/shard_map/pallas_call | solution.py:533
  43.6 18.5 %shard_map.113 = (bf16[64,512]{1,0:T(8,128)(2,1)}, bf16[32,1024]{1,0:T(8,128)(2,1)}, bf16[27,64,128]{2,1,0:T(8,128)(2,1)}) custom-call(bf16[64,512]{1,0:T(8,128)(2,1)} %get-tuple-element.6.a, bf16[32,1024]{1,0:T(8,128)(2,1)} %get-tuple-element.7.b, bf16[27,64,128]{2,1,0:T(8,128)(2,1)} %bitcast.5), custom_call_target="tpu_custom_call" | custom-call | tf_op jit(solution)/shard_map/pallas_call | solution.py:544

commit v4 on v3

--- a/solution.py
+++ b/solution.py
@@ -127,7 +127,7 @@
     padded = send.shape[2]
     blocks = pf.shape[0]
     groups = blocks // count
-    slice_rows = wnear.shape[1]
+    slice_rows = wfin.shape[0] // owners
     outer = owners // 2
     vox = lax.axis_index("vox")
     ch = lax.axis_index("ch")
@@ -253,7 +253,6 @@
         return carry
 
     lax.fori_loop(0, blocks, link, 0)
-    lax.fori_loop(0, offsets_all, ending, 0)
     for copy in copies:
         copy.wait()
 
@@ -282,6 +281,7 @@
     acc[...] = jnp.zeros_like(acc)
     prefix[0] = jnp.zeros_like(prefix[0])
     wsum[...] = jnp.zeros_like(wsum)
+    lax.fori_loop(0, offsets_all, ending, 0)
     for copy in copies:
         copy.wait()
 
@@ -312,58 +312,70 @@
         wsum[rows, :] = prefix[links[blocks + k]].astype(BF16)
         return carry
 
-    lax.fori_loop(0, offsets_all, pick, 0)
-
-    def slice_of(out_at, in_at):
-        first = (out_at * 2 + in_at) * slice_rows
-        return pl.ds(pl.multiple_of(first, 16), slice_rows)
+    lax.fori_loop(0, offsets_all, pick, 0, unroll=True)
+
+    part_rows = wnear.shape[2]
+    parts = slice_rows // part_rows
+
+    def piece(out_at, in_at, part):
+        first = (out_at * 2 + in_at) * slice_rows + part * part_rows
+        return pl.ds(pl.multiple_of(first, 16), part_rows)
 
     partner = mine_out * 2 + 1 - mine_in
     order = list(range(1, outer)) + [0]
     near = {}
-    for step in order:
-        to = lax.rem(mine_out + step, outer)
-        near[step] = pltpu.make_async_remote_copy(
-            src_ref=wsum.at[slice_of(to, 1 - mine_in)],
-            dst_ref=wnear.at[step],
-            send_sem=near_send.at[step],
-            recv_sem=near_recv.at[step],
-            device_id=(partner, ch),
-            device_id_type=MESH,
-        )
-        near[step].start()
+    for part in range(parts):
+        for step in order:
+            to = lax.rem(mine_out + step, outer)
+            near[part, step] = pltpu.make_async_remote_copy(
+                src_ref=wsum.at[piece(to, 1 - mine_in, part)],
+                dst_ref=wnear.at[part, step],
+                send_sem=near_send.at[part, step],
+                recv_sem=near_recv.at[part, step],
+                device_id=(partner, ch),
+                device_id_type=MESH,
+            )
+            near[part, step].start()
 
     def scatter(g, carry):
-        parts = []
+        terms = []
         for j in range(count):
             k = off[g * count + j]
-            parts.append(dot(ker[k], spread[g, :, j * LANES : (j + 1) * LANES], TN))
-        acc[...] += dot(split(jnp.concatenate(parts, axis=1)), foh[g], NT)
-        return carry
-
-    far = {}
+            terms.append(dot(ker[k], spread[g, :, j * LANES : (j + 1) * LANES], TN))
+        acc[...] += dot(split(jnp.concatenate(terms, axis=1)), foh[g], NT)
+        return carry
+
+    far, totals = {}, {}
+
+    def pass_on(part, step):
+        to = lax.rem(mine_out + step, outer)
+        near[part, step].wait()
+        both = wsum[piece(to, mine_in, part), :].astype(F32)
+        both = both + wnear[part, step].astype(F32)
+        if step == 0:
+            totals[part] = both
+            return
+        wpass[part, step] = both.astype(BF16)
+        far[part, step] = pltpu.make_async_remote_copy(
+            src_ref=wpass.at[part, step],
+            dst_ref=wfar.at[part, step],
+            send_sem=far_send.at[part, step],
+            recv_sem=far_recv.at[part, step],
+            device_id=(to * 2 + mine_in, ch),
+            device_id_type=MESH,
+        )
+        far[part, step].start()
+
     done = 0
     for number, step in enumerate(order):
         until = groups * (number + 1) // outer
         if until > done:
             lax.fori_loop(done, until, scatter, 0, unroll=True)
             done = until
-        to = lax.rem(mine_out + step, outer)
-        near[step].wait()
-        both = wsum[slice_of(to, mine_in), :].astype(F32) + wnear[step].astype(F32)
-        if step == 0:
-            total = both
-        else:
-            wpass[step] = both.astype(BF16)
-            far[step] = pltpu.make_async_remote_copy(
-                src_ref=wpass.at[step],
-                dst_ref=wfar.at[step],
-                send_sem=far_send.at[step],
-                recv_sem=far_recv.at[step],
-                device_id=(to * 2 + mine_in, ch),
-                device_id_type=MESH,
-            )
-            far[step].start()
+        pass_on(0, step)
+    for part in range(1, parts):
+        for step in order:
+            pass_on(part, step)
 
     share = width_in // channels
     mask_at = lax.broadcasted_iota(jnp.int32, (width_in, fine_total), 1)
@@ -385,12 +397,6 @@
         )
         fine[-1].start()
 
-    for step in order[:-1]:
-        far[step].wait()
-        total = total + wfar[step].astype(F32)
-    here = slice_of(mine_out, mine_in)
-    wfin[here, :] = (total * factor).astype(BF16)
-
     def finished(where, to, out_sem, in_sem_of):
         copy = pltpu.make_async_remote_copy(
             src_ref=wfin.at[where],
@@ -403,17 +409,36 @@
         copy.start()
         return copy
 
-    outward = [
-        finished(
-            here,
-            lax.rem(mine_out + step, outer) * 2 + mine_in,
-            out_send.at[step],
-            out_recv.at[step],
-        )
-        for step in range(1, outer)
-    ]
-    across = [finished(here, partner, fwd_send.at[0], fwd_recv.at[0])]
-
+    outward, across = {}, []
+    for part in range(parts):
+        total = totals[part]
+        for step in order[:-1]:
+            far[part, step].wait()
+            total = total + wfar[part, step].astype(F32)
+        here = piece(mine_out, mine_in, part)
+        wfin[here, :] = (total * factor).astype(BF16)
+        for step in range(1, outer):
+            outward[part, step] = finished(
+                here,
+                lax.rem(mine_out + step, outer) * 2 + mine_in,
+                out_send.at[part, step],
+                out_recv.at[part, step],
+            )
+        across.append(
+            finished(here, partner, fwd_send.at[part, 0], fwd_recv.at[part, 0])
+        )
+
+    def forward_on(part):
+        for step in range(1, outer):
+            outward[part, step].wait()
+            came = piece(lax.rem(mine_out + outer - step, outer), mine_in, part)
+            across.append(
+                finished(
+                    came, partner, fwd_send.at[part, step], fwd_recv.at[part, step]
+                )
+            )
+
+    forward_on(0)
     for copy in fine:
         copy.wait()
     kept = fsum[pl.ds(pl.multiple_of(ch * share, share), share), :]
@@ -422,11 +447,8 @@
     fine_here[...] = kept.astype(BF16)
     stores.append(pltpu.make_async_copy(fine_here, fine_out, end_sem.at[1]))
     stores[-1].start()
-
-    for step in range(1, outer):
-        outward[step - 1].wait()
-        came = slice_of(lax.rem(mine_out + outer - step, outer), mine_in)
-        across.append(finished(came, partner, fwd_send.at[step], fwd_recv.at[step]))
+    for part in range(1, parts):
+        forward_on(part)
     for copy in across:
         copy.wait()
 
@@ -436,15 +458,6 @@
     )
     stores[-1].start()
     for copy in stores:
-        copy.wait()
-
-
-def write_kernel(a, b, c, a_out, b_out, c_out, sem):
-    pairs = ((c, c_out), (a, a_out), (b, b_out))
-    copies = [pltpu.make_async_copy(x, y, sem.at[i]) for i, (x, y) in enumerate(pairs)]
-    for copy in copies:
-        copy.start()
-    for copy in copies:
         copy.wait()
 
 
@@ -472,6 +485,7 @@
     groups = blocks // count
     outer = owners // 2
     slice_rows = -(-offsets_all * width_out // (owners * 16)) * 16
+    parts = 2 if slice_rows % 32 == 0 else 1
     share = width_in // channels
     sm = pl.BlockSpec(memory_space=pltpu.SMEM)
     hbm = pl.BlockSpec(memory_space=pltpu.HBM)
@@ -517,9 +531,9 @@
         pltpu.VMEM((width_in, fine_total), BF16),
         pltpu.VMEM((channels, share, fine_total), BF16),
         pltpu.VMEM((owners * slice_rows, width_in), BF16),
-        pltpu.VMEM((outer, slice_rows, width_in), BF16),
-        pltpu.VMEM((outer, slice_rows, width_in), BF16),
-        pltpu.VMEM((outer, slice_rows, width_in), BF16),
+        pltpu.VMEM((parts, outer, slice_rows // parts, width_in), BF16),
+        pltpu.VMEM((parts, outer, slice_rows // parts, width_in), BF16),
+        pltpu.VMEM((parts, outer, slice_rows // parts, width_in), BF16),
         pltpu.VMEM((owners * slice_rows, width_in), BF16),
         dma((len(operands),)),
         dma((3,)),
@@ -529,7 +543,7 @@
         dma((owners,)),
         dma((channels,)),
         dma((channels,)),
-    ] + [dma((outer,)) for _ in range(8)]
+    ] + [dma((parts, outer)) for _ in range(8)]
     results = pl.pallas_call(
         functools.partial(whole_kernel, count, owners, channels, factor),
         out_shape=shapes[:2]
@@ -541,14 +555,7 @@
             collective_id=0, has_side_effects=True, vmem_limit_bytes=60 * 2**20
         ),
     )(block_offset, fine_count, *operands)
-    return pl.pallas_call(
-        write_kernel,
-        out_shape=shapes,
-        in_specs=[hbm, hbm, hbm],
-        out_specs=(hbm, hbm, hbm),
-        scratch_shapes=[dma((3,))],
-        compiler_params=pltpu.CompilerParams(vmem_limit_bytes=60 * 2**20),
-    )(results[0], results[1], results[2].reshape(kernel.shape))
+    return (results[0], results[1], results[2].reshape(kernel.shape))
 
 
 def solution(mesh):

time: 62.2 us -> 48.1 us (0.77)
  Pallas kernels: 60.8 us -> 42.6 us
  local copies, waits for them, and re-layouts: 0 us -> 3.94 us
    pallas_call x1 -> x0, Pallas kernels: 18.5 us -> none  [body(): pl.pallas_call(write_kernel, out_shape=shapes, in_specs=[hbm, hbm, hbm],...]
    unnamed x0 -> x5, local copies, waits for them, and re-layouts: none -> 3.94 us
where the time goes in v4:
time: 48.1 us; the launch traced here: 47.8 us
  Pallas kernels  42.6 us (89%)
  local copies, waits for them, and re-layouts  3.94 us (8%)
  between operations  1.3 us (3%)
    pallas_call x1, Pallas kernels, body(): pl.pallas_call(functools.partial(whole_kernel, count, owners, channels, f...  42.6 us
    unnamed x5, local copies, waits for them, and re-layouts  3.94 us

profile of v4, /device:TPU:0, one launch (start us, length us, event | category | flops | bytes accessed | tf_op | source)
XLA Modules:
  0.0 47.8 jit_solution(12826253000411048767)
XLA Ops:
  1.3 42.6 %shard_map.112 = (bf16[64,512]{1,0:T(8,128)(2,1)}, bf16[32,1024]{1,0:T(8,128)(2,1)}, bf16[1728,128]{1,0:T(8,128)(2,1)}) custom-call(s32[32]{0:T(128)} %off.1, s32[1]{0:T(128)S(6)} %copy.15.live, bf16[1024,128]{1,0:T(8,128)(2,1)} %feat_in.1, bf16[27,64,128]{2,1,0:T(8,128)(2,1)} %ker_in.1, bf16[64,512]{1,0:T(8,128)(2,1)} %cg_in.1, s32[32,128]{1,0:T(8,128)} %bitcast.6, ...), custom_call_target="tpu_custom_call" | custom-call | tf_op jit(solution)/shard_map/pallas_call | solution.py:547
  43.9 0.0 copy-start
  43.9 1.5 %copy.16 = bf16[64,512]{1,0:T(8,128)(2,1)} copy(bf16[64,512]{1,0:T(8,128)(2,1)} %get-tuple-element.12) | data formatting | bytes 131072
  45.4 0.0 copy-done
  45.4 0.6 %copy.17 = bf16[32,1024]{1,0:T(8,128)(2,1)} copy(bf16[32,1024]{1,0:T(8,128)(2,1)S(1)} %copy-done) | data formatting | bytes 131072
  46.0 1.8 %copy.18 = bf16[27,64,128]{2,1,0:T(8,128)(2,1)} copy(bf16[27,64,128]{2,1,0:T(8,128)(2,1)} %bitcast.5) | data formatting | bytes 884736
Async XLA Ops:
  43.9 1.5 %copy-start = (bf16[32,1024]{1,0:T(8,128)(2,1)S(1)}, bf16[32,1024]{1,0:T(8,128)(2,1)}, u32[]{:S(2)}) copy-start(bf16[32,1024]{1,0:T(8,128)(2,1)} %get-tuple-element.13) | copy-start | bytes 196612

commit v5 on v4

--- a/solution.py
+++ b/solution.py
@@ -278,7 +278,6 @@
     else:
         lax.fori_loop(0, owners, give, 0)
     copies = exchange(back, ret, b_send, b_recv)
-    acc[...] = jnp.zeros_like(acc)
     prefix[0] = jnp.zeros_like(prefix[0])
     wsum[...] = jnp.zeros_like(wsum)
     lax.fori_loop(0, offsets_all, ending, 0)
@@ -337,13 +336,18 @@
             )
             near[part, step].start()
 
-    def scatter(g, carry):
-        terms = []
-        for j in range(count):
-            k = off[g * count + j]
-            terms.append(dot(ker[k], spread[g, :, j * LANES : (j + 1) * LANES], TN))
-        acc[...] += dot(split(jnp.concatenate(terms, axis=1)), foh[g], NT)
-        return carry
+    pace = 2 if groups % 2 == 0 else 1
+
+    def scatter(turn):
+        more = None
+        for g in range(turn * pace, (turn + 1) * pace):
+            terms = []
+            for j in range(count):
+                rows = spread[g, :, j * LANES : (j + 1) * LANES]
+                terms.append(dot(ker[off[g * count + j]], rows, TN).astype(BF16))
+            added = dot(jnp.concatenate(terms, axis=1), foh[g], NT)
+            more = added if more is None else more + added
+        acc[...] = more if turn == 0 else acc[...] + more
 
     far, totals = {}, {}
 
@@ -366,36 +370,18 @@
         )
         far[part, step].start()
 
-    done = 0
-    for number, step in enumerate(order):
-        until = groups * (number + 1) // outer
-        if until > done:
-            lax.fori_loop(done, until, scatter, 0, unroll=True)
-            done = until
+    turns = groups // pace
+    scatter(0)
+    for step in order[:-1]:
         pass_on(0, step)
+    if turns > 1:
+        scatter(1)
+    pass_on(0, 0)
     for part in range(1, parts):
         for step in order:
             pass_on(part, step)
-
-    share = width_in // channels
-    mask_at = lax.broadcasted_iota(jnp.int32, (width_in, fine_total), 1)
-    whole = jnp.where(mask_at < live[0], joined(acc[...]), 0.0)
-    fsum[...] = whole
-    fsend[...] = whole.astype(BF16)
-    fine = []
-    for step in range(1, channels):
-        to = lax.rem(ch + step, channels)
-        fine.append(
-            pltpu.make_async_remote_copy(
-                src_ref=fsend.at[pl.ds(pl.multiple_of(to * share, share), share)],
-                dst_ref=frecv.at[step],
-                send_sem=f_send.at[step],
-                recv_sem=f_recv.at[step],
-                device_id=(vox, to),
-                device_id_type=MESH,
-            )
-        )
-        fine[-1].start()
+    for turn in range(2, turns - 1):
+        scatter(turn)
 
     def finished(where, to, out_sem, in_sem_of):
         copy = pltpu.make_async_remote_copy(
@@ -410,7 +396,8 @@
         return copy
 
     outward, across = {}, []
-    for part in range(parts):
+
+    def finish(part):
         total = totals[part]
         for step in order[:-1]:
             far[part, step].wait()
@@ -428,6 +415,31 @@
             finished(here, partner, fwd_send.at[part, 0], fwd_recv.at[part, 0])
         )
 
+    for part in range(parts):
+        finish(part)
+    if turns > 2:
+        scatter(turns - 1)
+
+    share = width_in // channels
+    mask_at = lax.broadcasted_iota(jnp.int32, (width_in, fine_total), 1)
+    whole = jnp.where(mask_at < live[0], acc[...], 0.0)
+    fsum[...] = whole
+    fsend[...] = whole.astype(BF16)
+    fine = []
+    for step in range(1, channels):
+        to = lax.rem(ch + step, channels)
+        fine.append(
+            pltpu.make_async_remote_copy(
+                src_ref=fsend.at[pl.ds(pl.multiple_of(to * share, share), share)],
+                dst_ref=frecv.at[step],
+                send_sem=f_send.at[step],
+                recv_sem=f_recv.at[step],
+                device_id=(vox, to),
+                device_id_type=MESH,
+            )
+        )
+        fine[-1].start()
+
     def forward_on(part):
         for step in range(1, outer):
             outward[part, step].wait()
@@ -459,6 +471,19 @@
     stores[-1].start()
     for copy in stores:
         copy.wait()
+
+
+def write_kernel(a, b, c, a_out, b_out, c_out, a_mid, b_mid, c_mid, in_sem, out_sem):
+    pairs = ((c, c_mid, c_out), (a, a_mid, a_out), (b, b_mid, b_out))
+    loads = [pltpu.make_async_copy(p[0], p[1], in_sem.at[i]) for i, p in enumerate(pairs)]
+    stores = [pltpu.make_async_copy(p[1], p[2], out_sem.at[i]) for i, p in enumerate(pairs)]
+    for load in loads:
+        load.start()
+    for load, store in zip(loads, stores):
+        load.wait()
+        store.start()
+    for store in stores:
+        store.wait()
 
 
 def body(
@@ -526,7 +551,7 @@
         pltpu.VMEM((owners, width_out, padded), BF16),
         pltpu.VMEM((blocks + 1, width_out, width_in), F32),
         pltpu.SMEM((blocks + offsets_all,), jnp.int32),
-        pltpu.VMEM((2 * width_in, fine_total), F32),
+        pltpu.VMEM((width_in, fine_total), F32),
         pltpu.VMEM((width_in, fine_total), F32),
         pltpu.VMEM((width_in, fine_total), BF16),
         pltpu.VMEM((channels, share, fine_total), BF16),
@@ -555,7 +580,14 @@
             collective_id=0, has_side_effects=True, vmem_limit_bytes=60 * 2**20
         ),
     )(block_offset, fine_count, *operands)
-    return (results[0], results[1], results[2].reshape(kernel.shape))
+    return pl.pallas_call(
+        write_kernel,
+        out_shape=shapes,
+        in_specs=[hbm, hbm, hbm],
+        out_specs=(hbm, hbm, hbm),
+        scratch_shapes=[pltpu.VMEM(a.shape, BF16) for a in shapes] + [dma((3,)), dma((3,))],
+        compiler_params=pltpu.CompilerParams(vmem_limit_bytes=60 * 2**20),
+    )(results[0], results[1], results[2].reshape(kernel.shape))
 
 
 def solution(mesh):

time: 48.1 us -> 46.6 us (0.969)
  local copies, waits for them, and re-layouts: 3.94 us -> 0 us
  Pallas kernels: 42.6 us -> 45.1 us
    unnamed x5 -> x0, local copies, waits for them, and re-layouts: 3.94 us -> none
    pallas_call x0 -> x1, Pallas kernels: none -> 1.86 us  [body(): pl.pallas_call(write_kernel, out_shape=shapes, in_specs=[hbm, hbm, hbm],...]
    pallas_call x1, Pallas kernels: 42.6 us -> 43.3 us  [body(): pl.pallas_call(functools.partial(whole_kernel, count, owners, channels, f...]
where the time goes in v5:
time: 46.6 us; the launch traced here: 46.4 us
  Pallas kernels  45.1 us (97%)
  between operations  1.29 us (3%)
    pallas_call x1, Pallas kernels, body(): pl.pallas_call(functools.partial(whole_kernel, count, owners, channels, f...  43.3 us
    pallas_call x1, Pallas kernels, body(): pl.pallas_call(write_kernel, out_shape=shapes, in_specs=[hbm, hbm, hbm],...  1.86 us

profile of v5, /device:TPU:0, one launch (start us, length us, event | category | flops | bytes accessed | tf_op | source)
XLA Modules:
  0.0 46.4 jit_solution(8266086583353463357)
XLA Ops:
  1.3 43.3 %shard_map.112 = (bf16[64,512]{1,0:T(8,128)(2,1)}, bf16[32,1024]{1,0:T(8,128)(2,1)}, bf16[1728,128]{1,0:T(8,128)(2,1)}) custom-call(s32[32]{0:T(128)} %off.1, s32[1]{0:T(128)S(6)} %copy.12.live, bf16[1024,128]{1,0:T(8,128)(2,1)} %feat_in.1, bf16[27,64,128]{2,1,0:T(8,128)(2,1)} %ker_in.1, bf16[64,512]{1,0:T(8,128)(2,1)} %cg_in.1, s32[32,128]{1,0:T(8,128)} %bitcast.6, ...), custom_call_target="tpu_custom_call" | custom-call | tf_op jit(solution)/shard_map/pallas_call | solution.py:572
  44.6 1.9 %shard_map.113 = (bf16[64,512]{1,0:T(8,128)(2,1)}, bf16[32,1024]{1,0:T(8,128)(2,1)}, bf16[27,64,128]{2,1,0:T(8,128)(2,1)}) custom-call(bf16[64,512]{1,0:T(8,128)(2,1)} %get-tuple-element.6.a, bf16[32,1024]{1,0:T(8,128)(2,1)} %get-tuple-element.7.b, bf16[27,64,128]{2,1,0:T(8,128)(2,1)} %bitcast.5), custom_call_target="tpu_custom_call" | custom-call | tf_op jit(solution)/shard_map/pallas_call | solution.py:583

commit v6 on v5

--- a/solution.py
+++ b/solution.py
@@ -60,7 +60,7 @@
     owners,
     channels,
     factor,
-    off,
+    off_in,
     live,
     feat_in,
     ker_in,
@@ -81,6 +81,7 @@
     pt,
     own,
     slots,
+    off,
     routes,
     places,
     ft,
@@ -146,6 +147,7 @@
     pairs = [
         (own_in, own),
         (slots_in, slots),
+        (off_in, off),
         (pf_in, pf),
         (pt_in, pt),
         (feat_in, feat),
@@ -174,7 +176,7 @@
                 pieces.append(blank)
             ids = jnp.concatenate(pieces, axis=1)
             places[:, o * padded : (o + 1) * padded] = onehot(coarse_total, ids)
-    for load in loads[2:6]:
+    for load in loads[2:7]:
         load.wait()
 
     at = lax.broadcasted_iota(jnp.int32, (fine_total, width_in), 0)
@@ -214,7 +216,7 @@
         apart(dot(part, routes[...], NT), send)
     else:
         lax.fori_loop(0, owners, route, 0)
-    loads[6].wait()
+    loads[7].wait()
 
     def exchange(source, target, out_sem, in_sem_of):
         copies = []
@@ -512,7 +514,6 @@
     slice_rows = -(-offsets_all * width_out // (owners * 16)) * 16
     parts = 2 if slice_rows % 32 == 0 else 1
     share = width_in // channels
-    sm = pl.BlockSpec(memory_space=pltpu.SMEM)
     hbm = pl.BlockSpec(memory_space=pltpu.HBM)
     pf = pair_fine.reshape(blocks, LANES)
     pt = pair_target.reshape(blocks, LANES)
@@ -538,6 +539,7 @@
     )
     scratch = [pltpu.VMEM(a.shape, BF16) for a in shapes[:2]]
     scratch += [pltpu.VMEM(a.shape, a.dtype) for a in operands] + [
+        pltpu.SMEM(block_offset.shape, jnp.int32),
         pltpu.VMEM((kept, targets), BF16),
         pltpu.VMEM((coarse_total, kept), BF16),
         pltpu.VMEM((width_in, fine_total), BF16),
@@ -560,7 +562,7 @@
         pltpu.VMEM((parts, outer, slice_rows // parts, width_in), BF16),
         pltpu.VMEM((parts, outer, slice_rows // parts, width_in), BF16),
         pltpu.VMEM((owners * slice_rows, width_in), BF16),
-        dma((len(operands),)),
+        dma((len(operands) + 1,)),
         dma((3,)),
         dma((owners,)),
         dma((owners,)),
@@ -573,7 +575,7 @@
         functools.partial(whole_kernel, count, owners, channels, factor),
         out_shape=shapes[:2]
         + (jax.ShapeDtypeStruct((offsets_all * width_out, width_in), BF16),),
-        in_specs=[sm, sm] + [hbm] * len(operands),
+        in_specs=[hbm, pl.BlockSpec(memory_space=pltpu.SMEM)] + [hbm] * len(operands),
         out_specs=(hbm, hbm, hbm),
         scratch_shapes=scratch,
         compiler_params=pltpu.CompilerParams(

time: 46.6 us -> 46.1 us (0.989)
  Pallas kernels: 45.1 us -> 44.6 us
    pallas_call x1, Pallas kernels: 43.3 us -> 42.7 us  [body(): pl.pallas_call(functools.partial(whole_kernel, count, owners, channels, f...]
where the time goes in v6:
time: 46.1 us; the launch traced here: 45.9 us
  Pallas kernels  44.6 us (97%)
  between operations  1.29 us (3%)
    pallas_call x1, Pallas kernels, body(): pl.pallas_call(functools.partial(whole_kernel, count, owners, channels, f...  42.7 us
    pallas_call x1, Pallas kernels, body(): pl.pallas_call(write_kernel, out_shape=shapes, in_specs=[hbm, hbm, hbm],...  1.86 us

profile of v6, /device:TPU:0, one launch (start us, length us, event | category | flops | bytes accessed | tf_op | source)
XLA Modules:
  0.0 45.9 jit_solution(12969147081470806463)
XLA Ops:
  1.3 42.7 %shard_map.112 = (bf16[64,512]{1,0:T(8,128)(2,1)}, bf16[32,1024]{1,0:T(8,128)(2,1)}, bf16[1728,128]{1,0:T(8,128)(2,1)}) custom-call(s32[32]{0:T(128)} %off_in.1, s32[1]{0:T(128)S(6)} %copy.12.live, bf16[1024,128]{1,0:T(8,128)(2,1)} %feat_in.1, bf16[27,64,128]{2,1,0:T(8,128)(2,1)} %ker_in.1, bf16[64,512]{1,0:T(8,128)(2,1)} %cg_in.1, s32[32,128]{1,0:T(8,128)} %bitcast.6, ...), custom_call_target="tpu_custom_call" | custom-call | tf_op jit(solution)/shard_map/pallas_call | solution.py:574
  44.0 1.9 %shard_map.113 = (bf16[64,512]{1,0:T(8,128)(2,1)}, bf16[32,1024]{1,0:T(8,128)(2,1)}, bf16[27,64,128]{2,1,0:T(8,128)(2,1)}) custom-call(bf16[64,512]{1,0:T(8,128)(2,1)} %get-tuple-element.6.a, bf16[32,1024]{1,0:T(8,128)(2,1)} %get-tuple-element.7.b, bf16[27,64,128]{2,1,0:T(8,128)(2,1)} %bitcast.5), custom_call_target="tpu_custom_call" | custom-call | tf_op jit(solution)/shard_map/pallas_call | solution.py:585
